TPU v7x, 32 devices: a whole 2x2x4 slice. The times are simulated.
32 devices in a mesh: row: 8 (over y, x, core), col: 4 (over z).
Axes of the slice: x: 2, y: 2, z: 4, core: 2. Of those that a mesh axis runs over, the one named last changes fastest.
Arguments:
- ensemble: float32 [4096, 1024], P(('row', 'col')), may hold values from -6 to 6
- obs_rows: int32 [2, 256], replicated, may hold values from 0 to 127
- owner: int32 [2], replicated, may hold values from 0 to 7
- obs_value: float32 [2, 256], replicated, may hold values from -8 to 8
- obs_var: float32 [2, 256], replicated, may hold values from 0.1 to 2
- taper_mask: int32 [2, 32, 2], P(None, ('row', 'col')), may hold values 0 or 1
Outputs:
- analysis: float32 [4096, 1024], P(('row', 'col'))
Inputs may be any that keep to these rules, and one draw needn't show every extreme that they name: `obs_rows`: observation p of batch b lies on the device at col index p // (256 / 4) of group owner[b]; batches may repeat a group and an observation may repeat a row.
All inputs are finite; a program needn't handle non-finite values. No bound on the sum of `taper_mask` on one device may be relied on, other than what follows from the above.
Results may differ from a plain program's by a relative error of at most 0.00018.
Values sent between devices are 32-bit elements; how exact they have to be, the bound alone decides.
A program may use at most 64 MiB of HBM per device.

v0:
```python
import functools

import jax
import jax.numpy as jnp
from jax import lax
from jax.experimental import pallas as pl
from jax.experimental.pallas import tpu as pltpu
from jax.sharding import PartitionSpec as P

W = 16
F32 = jnp.float32
BF16 = jnp.bfloat16
NN = (((1,), (0,)), ((), ()))
NT = (((1,), (1,)), ((), ()))
TN = (((0,), (0,)), ((), ()))


def split2(x):
    hi = x.astype(BF16)
    return hi, (x - hi.astype(F32)).astype(BF16)


def split3(x):
    hi = x.astype(BF16)
    rest = x - hi.astype(F32)
    mid = rest.astype(BF16)
    return hi, mid, (rest - mid.astype(F32)).astype(BF16)


def mm(a, b, dims):
    return lax.dot_general(a, b, dims, preferred_element_type=F32)


def dot3(a, b, dims):
    return mm(a[0], b[0], dims) + (mm(a[0], b[1], dims) + mm(a[1], b[0], dims))


def sweep_inverse(cov):
    size = cov.shape[0]
    lane = lax.broadcasted_iota(jnp.int32, (W, size), 1)
    row = lax.broadcasted_iota(jnp.int32, (W, size), 0)
    row_small = lax.broadcasted_iota(jnp.int32, (W, 128), 0)

    def body(k, carry):
        start = pl.multiple_of(k * W, W)
        panel = cov[pl.ds(start, W), :]
        rolled = pltpu.roll(panel, size - start, 1)
        cols = [jnp.broadcast_to(rolled[:, i:i + 1], (W, 128)) for i in range(W)]
        inside = (lane >= start) & (lane < start + W)
        left = jnp.where(inside, jnp.where(lane - start == row, -1.0, 0.0), panel)
        right = left
        scale = jnp.zeros((W, 128), F32)
        for j in range(W):
            inv = 1.0 / cols[j][j:j + 1, :]
            here = row_small == j
            mult = jnp.where(here, 0.0, cols[j])
            scale = jnp.where(here, inv, scale)
            for i in range(j + 1, W):
                cols[i] = cols[i] - mult * (cols[i][j:j + 1, :] * inv)
            wide = jnp.concatenate([mult] * (size // 128), axis=1)
            wide_inv = jnp.concatenate([inv] * (size // 128), axis=1)
            right = right - wide * (right[j:j + 1, :] * wide_inv)
        right = right * jnp.concatenate([scale] * (size // 128), axis=1)
        a1, a2, a3 = split3(left)
        b1, b2, b3 = split3(right)
        lhs = jnp.concatenate([a1, a1, a2, a1, a2, a3], axis=0)
        rhs = jnp.concatenate([b1, b2, b1, b3, b2, b1], axis=0)
        change = mm(lhs, rhs, TN)
        r_ids = lax.broadcasted_iota(jnp.int32, (size, size), 0)
        c_ids = lax.broadcasted_iota(jnp.int32, (size, size), 1)
        hit = ((r_ids >= start) & (r_ids < start + W)) | ((c_ids >= start) & (c_ids < start + W))
        cov[...] = jnp.where(hit, 0.0, cov[...]) - change
        return carry

    lax.fori_loop(0, size // W, body, 0)


def row_mean(x):
    return jnp.sum(x, axis=1, keepdims=True) * (1.0 / x.shape[1])


def covariance(anom2, var_ref, cov):
    size, members = anom2[0].shape
    r_ids = lax.broadcasted_iota(jnp.int32, (size, size), 0)
    c_ids = lax.broadcasted_iota(jnp.int32, (size, size), 1)
    full = dot3(anom2, anom2, NT) * (1.0 / (members - 1.0))
    cov[...] = full + jnp.where(r_ids == c_ids, jnp.broadcast_to(var_ref, (size, size)), 0.0)


def first_kernel(obs_ref, var_ref, out_ref):
    obs = obs_ref[...]
    covariance(split2(obs - row_mean(obs)), var_ref[...], out_ref)
    sweep_inverse(out_ref)


def taper_of(positions, glob, mask, local_len):
    dist = jnp.abs(positions - glob).astype(F32)
    return mask * jnp.exp(-dist / local_len)


def gain_step(anom2, obs2, neg_inv2, taper, members):
    cross = dot3(anom2, obs2, NT) * (1.0 / (members - 1.0))
    return dot3(split2(taper * cross), neg_inv2, NN)


def second_kernel(local_len, x_ref, g0_ref, g1_ref, inv_ref, glob_ref, gcol_ref, pos_ref, val_ref, var_ref,
                  mask0_ref, mask0g_ref, mask1_ref, out_ref, x1, g1, cov):
    members = x_ref.shape[1]
    rows = x_ref.shape[0]
    size = g0_ref.shape[0]
    g0 = g0_ref[...]
    m0 = row_mean(g0)
    a0 = g0 - m0
    a02 = split2(a0)
    inv2 = split2(inv_ref[...])
    push = split2(val_ref[:, 0:1] - m0 - 0.5 * a0)
    glob0 = glob_ref[0:1, :]
    glob1 = glob_ref[1:2, :]
    pos = pos_ref[...]
    for src, where, mask, dst in ((x_ref, pos, mask0_ref, x1), (g1_ref, gcol_ref[:, 1:2], mask0g_ref, g1)):
        x = src[...]
        taper = taper_of(where, glob0, mask[...], local_len)
        gain = split2(gain_step(split2(x - row_mean(x)), a02, inv2, taper, members))
        dst[...] = x - dot3(gain, push, NN)
    g = g1[...]
    m1 = row_mean(g)
    a1 = g - m1
    a12 = split2(a1)
    covariance(a12, var_ref[1:2, :], cov)
    sweep_inverse(cov)
    push = split2(val_ref[:, 1:2] - m1 - 0.5 * a1)
    x = x1[...]
    taper = taper_of(pos, glob1, mask1_ref[...], local_len)
    gain = split2(gain_step(split2(x - row_mean(x)), a12, split2(cov[...]), taper, members))
    out_ref[...] = x - dot3(gain, push, NN)


def on_device(ensemble, obs_rows, owner, obs_value, obs_var, taper_mask):
    rows, members = ensemble.shape
    batches, count = obs_rows.shape
    ncols = lax.axis_size("col")
    nrows = lax.axis_size("row")
    per_dev = count // ncols
    nblk = taper_mask.shape[2]
    local_len = float(rows * nrows * ncols // 4)
    my_row = lax.axis_index("row")
    my_col = lax.axis_index("col")
    first = (my_row * ncols + my_col) * rows
    row_ids = jnp.arange(rows, dtype=jnp.int32)
    column_of = jnp.arange(count, dtype=jnp.int32) // per_dev
    glob = (owner[:, None] * ncols + column_of[None, :]) * rows + obs_rows
    mine = lax.dynamic_slice_in_dim(obs_rows, my_col * per_dev, per_dev, axis=1)
    shared = []
    for batch in range(batches):
        here = (owner[batch] == my_row)
        picker = ((mine[batch][:, None] == row_ids[None, :]) & here).astype(F32)
        part = jnp.dot(picker, ensemble, precision=lax.Precision.HIGHEST)
        if batch == 1:
            note = jnp.where(here, taper_mask[0, 0].astype(F32), 0.0)
            note = jnp.pad(jnp.broadcast_to(note[None, :], (8, nblk)), ((0, 0), (0, members - nblk)))
            part = jnp.concatenate([part, note], axis=0)
        part = lax.psum(part, "row")
        shared.append(lax.all_gather(part, "col", axis=0))
    g0 = shared[0].reshape(count, members)
    g1 = shared[1][:, :per_dev].reshape(count, members)
    mask_g = jnp.repeat(shared[1][:, per_dev, :nblk], per_dev, axis=0)
    widen = lambda m: jnp.repeat(m.astype(F32), count // nblk, axis=-1)
    vmem = pl.BlockSpec(memory_space=pltpu.VMEM)
    inv = pl.pallas_call(
        first_kernel,
        out_shape=jax.ShapeDtypeStruct((count, count), F32),
        in_specs=[vmem] * 2,
        out_specs=vmem,
        compiler_params=pltpu.CompilerParams(vmem_limit_bytes=32 * 2**20),
        cost_estimate=pl.CostEstimate(flops=10**10, bytes_accessed=2**21, transcendentals=0),
    )(g0, obs_var[0:1])
    return pl.pallas_call(
        functools.partial(second_kernel, local_len),
        out_shape=jax.ShapeDtypeStruct((rows, members), F32),
        in_specs=[vmem] * 12,
        out_specs=vmem,
        scratch_shapes=[
            pltpu.VMEM((rows, members), F32),
            pltpu.VMEM((count, members), F32),
            pltpu.VMEM((count, count), F32),
        ],
        compiler_params=pltpu.CompilerParams(vmem_limit_bytes=40 * 2**20),
        cost_estimate=pl.CostEstimate(flops=2 * 10**10, bytes_accessed=2**22, transcendentals=0),
    )(
        ensemble, g0, g1, inv, glob, glob.T, (first + row_ids)[:, None], obs_value.T, obs_var,
        widen(taper_mask[0]), widen(mask_g), widen(taper_mask[1]),
    )


def solution(mesh):
    in_specs = (P(("row", "col"), None), P(), P(), P(), P(), P(None, ("row", "col"), None))
    out_specs = P(("row", "col"), None)
    return jax.shard_map(
        on_device, mesh=mesh, in_specs=in_specs, out_specs=out_specs, check_vma=False
    )
```

profile of v0, /device:TPU:0, one launch (start us, length us, event | category | flops | bytes accessed | tf_op | source)
XLA Modules:
  0.0 157.5 jit_solution(8371490078448858605)
XLA Ops:
  6.5 0.0 copy-start
  6.5 0.0 all-reduce.4.cloned.1.call-start
  6.5 0.8 constant_dynamic-slice_fusion
  7.4 1.3 fusion.9
  10.0 0.7 broadcast_select_fusion
  10.7 1.4 fusion.3
  12.1 0.0 copy-start.6
  12.1 0.0 copy-start.4
  12.1 0.0 copy-start.1
  12.1 0.7 maximum_bitcast_fusion
  12.9 0.0 copy-done
  12.9 0.0 copy-start.5
  12.9 0.0 copy-start.7
  12.9 1.0 convolution_bitcast_fusion
  13.9 0.0 all-reduce.4.cloned.1.call-update
  13.9 0.0 all-gather.3.cloned.1.call-start
  14.0 57.7 %all-reduce.4.cloned.1.call-done = (f32[1,64,1024]{2,1,0:T(8,128)}, f32[1,72,1024]{2,1,0:T(8,128)}) async-done(((f32[1,64,1024]{2,1,0:T(8,128)}, f32[1,72,1024]{2,1,0:T(8,128)}), (f32[1,64,1024]{2,1,0:T(8,128)}, f32[1,72,1024]{2,1,0:T(8,128)})) %all-reduce.4.cloned.1.call-update) | async-done | bytes 557072 | tf_op jit(solution)/shard_map/psum | solution.py:162
  71.7 0.0 all-gather.3.cloned.1.call-update
  71.7 0.0 all-gather.5.cloned.1.call-start
  71.7 0.0 copy-done.6
  71.8 0.7 all-gather.5.cloned.1.call-update
  72.4 0.0 copy-done.4
  72.4 0.1 copy.18
  72.6 0.0 copy-done.1
  72.6 0.1 multiply_add_fusion
  72.7 0.1 copy.22.glob_ref
  72.8 0.0 copy-done.5
  72.8 0.1 copy.19
  73.0 0.0 copy-done.7
  73.0 0.1 fusion.12.gcol_ref
  73.1 27.6 %all-gather.3.cloned.1.call-done = f32[4,64,1024]{2,1,0:T(8,128)} async-done(((f32[1,64,1024]{2,1,0:T(8,128)}), f32[4,64,1024]{2,1,0:T(8,128)}) %all-gather.3.cloned.1.call-update) | async-done | bytes 1048592 | tf_op jit(solution)/shard_map/all_gather | solution.py:163
  100.7 0.0 copy-start.2
  100.7 1.2 copy-done.2
  102.0 9.5 %shard_map.64.inv_ref = f32[256,256]{1,0:T(8,128)S(1)} custom-call(f32[256,1024]{1,0:T(8,128)S(1)} %bitcast.34, f32[1,256]{1,0:T(1,128)S(1)} %slice.34.var_ref), custom_call_target="tpu_custom_call" | custom-call | flops 10000000000 | bytes 2097152 | tf_op jit(solution)/shard_map/pallas_call | solution.py:169
  111.5 21.0 %all-gather.5.cloned.1.call-done = f32[4,72,1024]{2,1,0:T(8,128)} async-done(((f32[1,72,1024]{2,1,0:T(8,128)}), f32[4,72,1024]{2,1,0:T(8,128)}) %all-gather.5.cloned.1.call-update) | async-done | bytes 1179664 | tf_op jit(solution)/shard_map/all_gather | solution.py:163
  132.4 0.7 slice.38
  133.1 0.3 broadcast_in_dim.33
  133.5 0.0 copy-start.3
  133.5 1.4 slice.37
  134.9 0.1 broadcast_in_dim.30
  135.0 0.1 broadcast_in_dim.34
  135.1 0.0 copy-done.3
  135.1 15.9 %shard_map.65 = f32[128,1024]{1,0:T(8,128)} custom-call(f32[128,1024]{1,0:T(8,128)S(1)} %copy-done, f32[256,1024]{1,0:T(8,128)S(1)} %bitcast.35, f32[256,1024]{1,0:T(8,128)S(1)} %bitcast.31, f32[256,256]{1,0:T(8,128)S(1)} %shard_map.64.inv_ref, s32[2,256]{1,0:T(2,128)S(1)} %copy.22.glob_ref, s32[256,2]{1,0:T(8,128)S(1)} %fusion.12.gcol_ref, ...), custom_call_target="tpu_custom_call" | custom-call | flops 20000000000 | bytes 4194304 | tf_op jit(solution)/shard_map/pallas_call | solution.py:177
  (10 shorter events, 0.1 us)
Async XLA Ops:
  6.5 6.3 %copy-start = (f32[128,1024]{1,0:T(8,128)S(1)}, f32[128,1024]{1,0:T(8,128)}, u32[]{:S(2)}) copy-start(f32[128,1024]{1,0:T(8,128)} %x_ref.1) | copy-start | bytes 1572868
  6.5 65.1 %all-reduce.4.cloned.1.call-start = ((), (), s32[]{:S(2)}) async-start(), calls=%async_computation.2 | async-start | bytes 1114112 | tf_op jit(solution)/shard_map/psum | solution.py:162
  12.1 59.7 %copy-start.6 = (s32[2]{0:T(128)S(1)}, s32[2]{0:T(128)}, u32[]{:S(2)}) copy-start(s32[2]{0:T(128)} %param.8) | copy-start | bytes 28
  12.1 60.3 %copy-start.4 = (s32[2,256]{1,0:T(2,128)S(1)}, s32[2,256]{1,0:T(2,128)}, u32[]{:S(2)}) copy-start(s32[2,256]{1,0:T(2,128)} %param.7) | copy-start | bytes 6148
  12.1 60.5 %copy-start.1 = (f32[2,256]{1,0:T(2,128)S(1)}, f32[2,256]{1,0:T(2,128)}, u32[]{:S(2)}) copy-start(f32[2,256]{1,0:T(2,128)} %var_ref.1) | copy-start | bytes 6148
  12.9 59.9 %copy-start.5 = (f32[2,256]{1,0:T(2,128)S(1)}, f32[2,256]{1,0:T(2,128)}, u32[]{:S(2)}) copy-start(f32[2,256]{1,0:T(2,128)} %param.9) | copy-start | bytes 6148
  12.9 60.1 %copy-start.7 = (s32[2,1,2]{2,1,0:T(1,128)S(1)}, s32[2,1,2]{2,1,0:T(1,128)}, u32[]{:S(2)}) copy-start(s32[2,1,2]{2,1,0:T(1,128)} %param.11) | copy-start | bytes 52
  13.9 86.8 %all-gather.3.cloned.1.call-start = ((), (), s32[]{:S(2)}) async-start(), calls=%async_computation | async-start | bytes 1310720 | tf_op jit(solution)/shard_map/all_gather | solution.py:163
  71.7 60.7 %all-gather.5.cloned.1.call-start = ((), (), s32[]{:S(2)}) async-start(), calls=%async_computation.1 | async-start | bytes 1474560 | tf_op jit(solution)/shard_map/all_gather | solution.py:163
  100.7 1.2 copy-start.2
  133.5 1.6 %copy-start.3 = (f32[4,64,1024]{2,1,0:T(8,128)S(1)}, f32[4,64,1024]{2,1,0:T(8,128)}, u32[]{:S(2)}) copy-start(f32[4,64,1024]{2,1,0:T(8,128)} %all-gather.3.cloned.1.call-done) | copy-start | bytes 3145732
Sparse Core Ops, SparseCore 0:
  14.1 57.5 all-reduce.3
  73.3 27.3 all-gather.2
  102.4 29.9 all-gather.4
where the time goes:
time: 158 us; the launch traced here: 157 us
  waiting for transfers between devices  107 us (68%)
  Pallas kernels  25.4 us (16%)
  between operations  14.7 us (9%)
  local copies, waits for them, and re-layouts  6.39 us (4%)
  matrix products  2.42 us (2%)
  other arithmetic  1.61 us (1%)
    psum x1, waiting for transfers between devices, on_device(): part = lax.psum(part, 'row')  57.7 us
    all_gather x2, waiting for transfers between devices, on_device(): shared.append(lax.all_gather(part, 'col', axis=0))  48.6 us
    pallas_call x1, Pallas kernels, on_device(): pl.pallas_call(functools.partial(second_kernel, local_len), out_shape=jax...  15.9 us
    pallas_call x1, Pallas kernels, on_device(): pl.pallas_call(first_kernel, out_shape=jax.ShapeDtypeStruct((count, count...  9.49 us
  transfers between devices with their start and end apart: 3, of which 3 were waited for; matrix products, arithmetic and copies ran while one was open for 0% of the time, Pallas kernels for 6%

commit v1 on v0

v1 whole, which is shorter than its diff:
```python
import functools

import jax
import jax.numpy as jnp
from jax import lax
from jax.experimental import pallas as pl
from jax.experimental.pallas import tpu as pltpu
from jax.sharding import PartitionSpec as P

W = 16
F32 = jnp.float32
BF16 = jnp.bfloat16
NN = (((1,), (0,)), ((), ()))
NT = (((1,), (1,)), ((), ()))
TN = (((0,), (0,)), ((), ()))
MESH = pl.DeviceIdType.MESH
VMEM = pl.BlockSpec(memory_space=pltpu.VMEM)
SMEM = pl.BlockSpec(memory_space=pltpu.SMEM)


def split2(x):
    hi = x.astype(BF16)
    return hi, (x - hi.astype(F32)).astype(BF16)


def split3(x):
    hi = x.astype(BF16)
    rest = x - hi.astype(F32)
    mid = rest.astype(BF16)
    return hi, mid, (rest - mid.astype(F32)).astype(BF16)


def mm(a, b, dims):
    return lax.dot_general(a, b, dims, preferred_element_type=F32)


def dot3(a, b, dims):
    return mm(a[0], b[0], dims) + (mm(a[0], b[1], dims) + mm(a[1], b[0], dims))


def sweep_inverse(cov):
    size = cov.shape[0]
    lane = lax.broadcasted_iota(jnp.int32, (W, size), 1)
    row = lax.broadcasted_iota(jnp.int32, (W, size), 0)
    row_small = lax.broadcasted_iota(jnp.int32, (W, 128), 0)

    def body(k, carry):
        start = pl.multiple_of(k * W, W)
        panel = cov[pl.ds(start, W), :]
        rolled = pltpu.roll(panel, size - start, 1)
        cols = [jnp.broadcast_to(rolled[:, i:i + 1], (W, 128)) for i in range(W)]
        inside = (lane >= start) & (lane < start + W)
        left = jnp.where(inside, jnp.where(lane - start == row, -1.0, 0.0), panel)
        right = left
        scale = jnp.zeros((W, 128), F32)
        for j in range(W):
            inv = 1.0 / cols[j][j:j + 1, :]
            here = row_small == j
            mult = jnp.where(here, 0.0, cols[j])
            scale = jnp.where(here, inv, scale)
            for i in range(j + 1, W):
                cols[i] = cols[i] - mult * (cols[i][j:j + 1, :] * inv)
            wide = jnp.concatenate([mult] * (size // 128), axis=1)
            wide_inv = jnp.concatenate([inv] * (size // 128), axis=1)
            right = right - wide * (right[j:j + 1, :] * wide_inv)
        right = right * jnp.concatenate([scale] * (size // 128), axis=1)
        a1, a2, a3 = split3(left)
        b1, b2, b3 = split3(right)
        lhs = jnp.concatenate([a1, a1, a2, a1, a2, a3], axis=0)
        rhs = jnp.concatenate([b1, b2, b1, b3, b2, b1], axis=0)
        change = mm(lhs, rhs, TN)
        r_ids = lax.broadcasted_iota(jnp.int32, (size, size), 0)
        c_ids = lax.broadcasted_iota(jnp.int32, (size, size), 1)
        hit = ((r_ids >= start) & (r_ids < start + W)) | ((c_ids >= start) & (c_ids < start + W))
        cov[...] = jnp.where(hit, 0.0, cov[...]) - change
        return carry

    lax.fori_loop(0, size // W, body, 0)


def row_mean(x):
    return jnp.sum(x, axis=1, keepdims=True) * (1.0 / x.shape[1])


def covariance(anom2, var_ref, cov):
    size, members = anom2[0].shape
    r_ids = lax.broadcasted_iota(jnp.int32, (size, size), 0)
    c_ids = lax.broadcasted_iota(jnp.int32, (size, size), 1)
    full = dot3(anom2, anom2, NT) * (1.0 / (members - 1.0))
    cov[...] = full + jnp.where(r_ids == c_ids, jnp.broadcast_to(var_ref, (size, size)), 0.0)


def inverse_of(obs, var_row, cov):
    covariance(split2(obs - row_mean(obs)), var_row, cov)
    sweep_inverse(cov)


def first_kernel(obs_ref, var_ref, out_ref):
    inverse_of(obs_ref[...], var_ref[0:1, :], out_ref)


def share_kernel(nrows, ncols, x_ref, rows_ref, owner_ref, mask_ref, var_ref, g_ref, note_ref, inv_ref,
                 src, slots, note_src, note_slots, sum_s, sum_r, line_s, line_r, plane_s, plane_r, pair_s, pair_r,
                 nsum_s, nsum_r, nline_s, nline_r):
    me = lax.axis_index("row")
    col = lax.axis_index("col")
    nstate, members = x_ref.shape
    count = rows_ref.shape[1]
    per_dev = count // ncols
    q = per_dev // nrows
    half = nrows // 2
    sibling = me + 1 - 2 * (me % 2)

    barrier = pltpu.get_barrier_semaphore()
    for d in range(1, nrows):
        pl.semaphore_signal(barrier, inc=1, device_id=((me + d) % nrows, col), device_id_type=MESH)
    for d in range(1, ncols):
        pl.semaphore_signal(barrier, inc=1, device_id=(me, (col + d) % ncols), device_id_type=MESH)

    def put(source, target, send, recv, row, column):
        copy = pltpu.make_async_remote_copy(
            src_ref=source, dst_ref=target, send_sem=send, recv_sem=recv,
            device_id=(row, column), device_id_type=MESH)
        copy.start()
        return copy

    x3 = split3(x_ref[...])
    state_ids = lax.broadcasted_iota(jnp.int32, (nstate, per_dev), 0)
    sent = []

    def select(b):
        ids = jnp.broadcast_to(rows_ref[b:b + 1, :], (8, count))
        ids = pltpu.roll(ids, (count - col * per_dev) % count, 1)[0:1, :per_dev]
        here = jnp.full((1, per_dev), owner_ref[b], jnp.int32) == me
        ids = jnp.where(here, ids, -1)
        pick = jnp.where(ids == state_ids, 1.0, 0.0).astype(BF16)
        src[b] = (mm(pick, x3[0], TN) + mm(pick, x3[1], TN)) + mm(pick, x3[2], TN)

    def scatter(b):
        copies = []
        for d in range(1, nrows):
            peer = (me + d) % nrows
            copies.append(put(src.at[b, pl.ds(pl.multiple_of(peer * q, q), q)], slots.at[b, d - 1],
                              sum_s.at[b, d - 1], sum_r.at[b, d - 1], peer, col))
        sent.extend(copies)
        return copies

    def along_line(b, copies):
        for copy in copies:
            copy.wait_recv()
        total = src[b, pl.ds(pl.multiple_of(me * q, q), q), :]
        for d in range(1, nrows):
            total = total + slots[b, d - 1]
        g_ref[b, col, me] = total
        mine = g_ref.at[b, col, me]
        copies = [put(mine, mine, line_s.at[b, d - 1], line_r.at[b, d - 1], me, (col + d) % ncols)
                  for d in range(1, ncols)]
        sent.extend(copies)
        return copies

    def spread(b, d):
        slab = g_ref.at[b, (col + ncols - d) % ncols, me]
        copies = [put(slab, slab, plane_s.at[b, d, c - 1], plane_r.at[b, d, c - 1], (me + 2 * c) % nrows, col)
                  for c in range(1, half)]
        pairs = [put(slab, slab, pair_s.at[b, d, 0], pair_r.at[b, d, 0], sibling, col)]
        sent.extend(copies + pairs)
        return copies, pairs

    def in_plane(b, lines, first):
        planes, pairs = [first[0]], list(first[1])
        for d in range(1, ncols):
            lines[d - 1].wait_recv()
            more = spread(b, d)
            planes.append(more[0])
            pairs.extend(more[1])
        return planes, pairs

    def in_chip(b, planes, pairs):
        for d in range(ncols):
            for c in range(1, half):
                planes[d][c - 1].wait_recv()
                slab = g_ref.at[b, (col + ncols - d) % ncols, (me + nrows - 2 * c) % nrows]
                pairs.append(put(slab, slab, pair_s.at[b, d, c], pair_r.at[b, d, c], sibling, col))
                sent.append(pairs[-1])
        for copy in pairs:
            copy.wait_recv()

    lane = lax.broadcasted_iota(jnp.int32, (8, 128), 1)
    note = jnp.zeros((8, 128), F32)
    for j in range(mask_ref.shape[2]):
        note = jnp.where(lane == j, mask_ref[0, 0, j].astype(F32), note)
    here = jnp.full((8, 128), owner_ref[1], jnp.int32) == me
    note_src[...] = jnp.where(here, note, 0.0)
    select(0)
    pl.semaphore_wait(barrier, nrows + ncols - 2)
    sums0 = scatter(0)
    select(1)
    lines0 = along_line(0, sums0)
    first0 = spread(0, 0)
    notes = [put(note_src, note_slots.at[d - 1], nsum_s.at[d - 1], nsum_r.at[d - 1], (me + d) % nrows, col)
             for d in range(1, nrows)]
    planes0, pairs0 = in_plane(0, lines0, first0)
    sums1 = scatter(1)
    in_chip(0, planes0, pairs0)

    lines1 = along_line(1, sums1)
    first1 = spread(1, 0)
    total = note_src[...]
    for d in range(1, nrows):
        notes[d - 1].wait_recv()
        total = total + note_slots[d - 1]
    note_ref[col] = total
    note_lines = [put(note_ref.at[col], note_ref.at[col], nline_s.at[d - 1], nline_r.at[d - 1], me, (col + d) % ncols)
                  for d in range(1, ncols)]
    obs = g_ref[0].reshape(count, members)
    covariance(split2(obs - row_mean(obs)), var_ref[0:1, :], inv_ref)
    planes1, pairs1 = in_plane(1, lines1, first1)
    sweep_inverse(inv_ref)
    in_chip(1, planes1, pairs1)
    for copy in note_lines:
        copy.wait_recv()
    for copy in sent + notes + note_lines:
        copy.wait_send()


def column_of(row, eye):
    return jnp.sum(jnp.where(eye, jnp.broadcast_to(row, eye.shape), 0.0), axis=1, keepdims=True)


def gain_step(anom2, obs2, neg_inv2, taper, members):
    cross = dot3(anom2, obs2, NT) * (1.0 / (members - 1.0))
    return dot3(split2(taper * cross), neg_inv2, NN)


def second_kernel(nrows, ncols, x_ref, g_ref, inv_ref, note_ref, rows_ref, owner_ref, val_ref, var_ref, mask_ref,
                  out_ref, x1, g1, cov):
    rows, members = x_ref.shape
    count = rows_ref.shape[1]
    per_dev = count // ncols
    nblk = mask_ref.shape[2]
    wide = count // nblk
    local_len = float(rows * nrows * ncols // 4)
    eye = (lax.broadcasted_iota(jnp.int32, (count, count), 0)
           == lax.broadcasted_iota(jnp.int32, (count, count), 1))
    lane = lax.broadcasted_iota(jnp.int32, (1, count), 1)
    device = jnp.zeros((1, count), jnp.int32)
    for c in range(1, ncols):
        device = device + jnp.where(lane >= c * per_dev, 1, 0)
    glob = [((owner_ref[b] * ncols + device) * rows + rows_ref[b:b + 1, :]).astype(F32) for b in range(2)]
    first = (lax.axis_index("row") * ncols + lax.axis_index("col")) * rows
    pos = (first + lax.broadcasted_iota(jnp.int32, (rows, count), 0)).astype(F32)

    def widen(values):
        out = jnp.zeros((1, count), F32)
        for j, value in enumerate(values):
            out = jnp.where((lane >= j * wide) & (lane < (j + 1) * wide), value, out)
        return out

    def taper_of(position, where, mask):
        return mask * jnp.exp(-jnp.abs(position - where) / local_len)

    mask = [widen([mask_ref[b, 0, j].astype(F32) for j in range(nblk)]) for b in range(2)]
    mask_g = jnp.concatenate(
        [jnp.broadcast_to(widen([note_ref[c, 0:1, j:j + 1] for j in range(nblk)]), (per_dev, count))
         for c in range(ncols)], axis=0)
    gcol = column_of(glob[1], eye)

    g0 = g_ref[0].reshape(count, members)
    m0 = row_mean(g0)
    a0 = g0 - m0
    a02 = split2(a0)
    inv2 = split2(inv_ref[...])
    push = split2(column_of(val_ref[0:1, :], eye) - m0 - 0.5 * a0)
    for src, where, held, dst in ((g_ref[1].reshape(count, members), gcol, mask_g, g1),
                                  (x_ref[...], pos, mask[0], x1)):
        taper = taper_of(where, glob[0], held)
        gain = split2(gain_step(split2(src - row_mean(src)), a02, inv2, taper, members))
        dst[...] = src - dot3(gain, push, NN)
    g = g1[...]
    m1 = row_mean(g)
    a1 = g - m1
    a12 = split2(a1)
    covariance(a12, var_ref[1:2, :], cov)
    sweep_inverse(cov)
    push = split2(column_of(val_ref[1:2, :], eye) - m1 - 0.5 * a1)
    x = x1[...]
    taper = taper_of(pos, glob[1], mask[1])
    gain = split2(gain_step(split2(x - row_mean(x)), a12, split2(cov[...]), taper, members))
    out_ref[...] = x - dot3(gain, push, NN)


def shared_by_collectives(ensemble, obs_rows, owner, taper_mask, ncols):
    rows, members = ensemble.shape
    batches, count = obs_rows.shape
    per_dev = count // ncols
    nblk = taper_mask.shape[2]
    my_row = lax.axis_index("row")
    mine = lax.dynamic_slice_in_dim(obs_rows, lax.axis_index("col") * per_dev, per_dev, axis=1)
    row_ids = jnp.arange(rows, dtype=jnp.int32)
    shared = []
    for batch in range(batches):
        here = owner[batch] == my_row
        picker = ((mine[batch][:, None] == row_ids[None, :]) & here).astype(F32)
        part = jnp.dot(picker, ensemble, precision=lax.Precision.HIGHEST)
        shared.append(lax.all_gather(lax.psum(part, "row"), "col", axis=0).reshape(count, members))
    note = jnp.where(owner[1] == my_row, taper_mask[0, 0].astype(F32), 0.0)
    note = jnp.pad(jnp.broadcast_to(note[None, :], (8, nblk)), ((0, 0), (0, 128 - nblk)))
    note = lax.all_gather(lax.psum(note, "row"), "col", axis=0)
    return jnp.stack(shared), note


def on_device(nrows, ncols, ensemble, obs_rows, owner, obs_value, obs_var, taper_mask):
    rows, members = ensemble.shape
    batches, count = obs_rows.shape
    per_dev = count // ncols
    inv_shape = jax.ShapeDtypeStruct((count, count), F32)
    if per_dev % (8 * nrows) == 0 and nrows % 2 == 0:
        q = per_dev // nrows
        half = nrows // 2
        dma = pltpu.SemaphoreType.DMA
        shared, note, inv = pl.pallas_call(
            functools.partial(share_kernel, nrows, ncols),
            out_shape=(
                jax.ShapeDtypeStruct((batches, ncols, nrows, q, members), F32),
                jax.ShapeDtypeStruct((ncols, 8, 128), F32),
                inv_shape,
            ),
            in_specs=[VMEM, VMEM, SMEM, SMEM, VMEM],
            out_specs=(VMEM, VMEM, VMEM),
            scratch_shapes=[
                pltpu.VMEM((batches, per_dev, members), F32),
                pltpu.VMEM((batches, nrows - 1, q, members), F32),
                pltpu.VMEM((8, 128), F32),
                pltpu.VMEM((nrows - 1, 8, 128), F32),
            ] + [dma((batches, nrows - 1))] * 2 + [dma((batches, ncols - 1))] * 2
            + [dma((batches, ncols, half - 1))] * 2 + [dma((batches, ncols, half))] * 2
            + [dma((nrows - 1,))] * 2 + [dma((ncols - 1,))] * 2,
            compiler_params=pltpu.CompilerParams(
                vmem_limit_bytes=40 * 2**20, collective_id=0, has_side_effects=True),
        )(ensemble, obs_rows, owner, taper_mask, obs_var)
    else:
        shared, note = shared_by_collectives(ensemble, obs_rows, owner, taper_mask, ncols)
        inv = pl.pallas_call(
            first_kernel,
            out_shape=inv_shape,
            in_specs=[VMEM] * 2,
            out_specs=VMEM,
            compiler_params=pltpu.CompilerParams(vmem_limit_bytes=40 * 2**20),
        )(shared[0], obs_var)
    return pl.pallas_call(
        functools.partial(second_kernel, nrows, ncols),
        out_shape=jax.ShapeDtypeStruct((rows, members), F32),
        in_specs=[VMEM] * 5 + [SMEM, VMEM, VMEM, SMEM],
        out_specs=VMEM,
        scratch_shapes=[
            pltpu.VMEM((rows, members), F32),
            pltpu.VMEM((count, members), F32),
            pltpu.VMEM((count, count), F32),
        ],
        compiler_params=pltpu.CompilerParams(vmem_limit_bytes=40 * 2**20),
    )(ensemble, shared, inv, note, obs_rows, owner, obs_value, obs_var, taper_mask)


def solution(mesh):
    in_specs = (P(("row", "col"), None), P(), P(), P(), P(), P(None, ("row", "col"), None))
    out_specs = P(("row", "col"), None)
    return jax.shard_map(
        functools.partial(on_device, mesh.shape["row"], mesh.shape["col"]),
        mesh=mesh, in_specs=in_specs, out_specs=out_specs, check_vma=False
    )
```

time: 158 us -> 59 us (0.37)
  waiting for transfers between devices: 107 us -> 0 us
  Pallas kernels: 25.4 us -> 54.3 us
  between operations: 14.7 us -> 0.02 us
  matrix products: 2.42 us -> 0 us
  local copies, waits for them, and re-layouts: 6.39 us -> 4.41 us
  other arithmetic: 1.61 us -> 0 us
    psum x1 -> x0, waiting for transfers between devices: 57.7 us -> none  [on_device(): part = lax.psum(part, 'row')]
    all_gather x2 -> x0, waiting for transfers between devices: 48.6 us -> none  [on_device(): shared.append(lax.all_gather(part, 'col', axis=0))]
    pallas_call x2, Pallas kernels: 25.4 us -> 54.3 us  [the longest x1 38.5 us: on_device(): pl.pallas_call(functools.partial(share_kernel, nrows, ncols), out_shape=(...]
    slice x4 -> x0, local copies, waits for them, and re-layouts: 3.46 us -> none  [the longest x1 1.42 us: on_device(): g1 = shared[1][:, :per_dev].reshape(count, members)]
    unnamed x19 -> x12, local copies, waits for them, and re-layouts: 1.56 us -> 4.41 us
    dot_general x2 -> x0, matrix products: 2.42 us -> none  [on_device(): part = jnp.dot(picker, ensemble, precision=lax.Precision.HIGHEST)]
  transfers between devices with their start and end apart: 3 -> 0, of which waited for: 3 -> 0; matrix products, arithmetic and copies ran while one was open for 0% -> 0% of each run, Pallas kernels for 6% -> 0%
where the time goes in v1:
time: 59 us; the launch traced here: 58.7 us
  Pallas kernels  54.3 us (92%)
  local copies, waits for them, and re-layouts  4.41 us (7%)
    pallas_call x1, Pallas kernels, on_device(): pl.pallas_call(functools.partial(share_kernel, nrows, ncols), out_shape=(...  38.5 us
    pallas_call x1, Pallas kernels, on_device(): pl.pallas_call(functools.partial(second_kernel, nrows, ncols), out_shape=...  15.7 us
    unnamed x12, local copies, waits for them, and re-layouts  4.41 us

profile of v1, /device:TPU:0, one launch (start us, length us, event | category | flops | bytes accessed | tf_op | source)
XLA Modules:
  0.0 58.7 jit_solution(7319330900706671164)
XLA Ops:
  0.0 0.0 copy-start
  0.0 1.0 %copy-done = f32[128,1024]{1,0:T(8,128)S(1)} copy-done((f32[128,1024]{1,0:T(8,128)S(1)}, f32[128,1024]{1,0:T(8,128)}, u32[]{:S(2)}) %copy-start) | copy-done | bytes 524312
  1.0 0.0 copy-start.1
  1.0 0.7 %copy-done.1 = s32[2,256]{1,0:T(2,128)S(1)} copy-done((s32[2,256]{1,0:T(2,128)S(1)}, s32[2,256]{1,0:T(2,128)}, u32[]{:S(2)}) %copy-start.1) | copy-done | bytes 2072
  1.7 0.0 copy-start.2
  1.7 0.7 %copy-done.2 = f32[2,256]{1,0:T(2,128)S(1)} copy-done((f32[2,256]{1,0:T(2,128)S(1)}, f32[2,256]{1,0:T(2,128)}, u32[]{:S(2)}) %copy-start.2) | copy-done | bytes 2072
  2.4 0.0 copy-start.3
  2.4 0.7 %copy-done.3 = s32[2,1,2]{2,1,0:T(1,128)S(1)} copy-done((s32[2,1,2]{2,1,0:T(1,128)S(1)}, s32[2,1,2]{2,1,0:T(1,128)}, u32[]{:S(2)}) %copy-start.3) | copy-done | bytes 40
  3.1 0.0 copy-start.5
  3.1 0.7 %copy-done.5 = s32[2]{0:T(128)S(1)} copy-done((s32[2]{0:T(128)S(1)}, s32[2]{0:T(128)}, u32[]{:S(2)}) %copy-start.5) | copy-done | bytes 32
  3.7 38.5 %shard_map.64 = (f32[2,4,8,8,1024]{4,3,2,1,0:T(8,128)S(1)}, f32[4,8,128]{2,1,0:T(8,128)S(1)}, f32[256,256]{1,0:T(8,128)S(1)}) custom-call(f32[128,1024]{1,0:T(8,128)S(1)} %copy-done, s32[2,256]{1,0:T(2,128)S(1)} %copy-done.1, s32[2]{0:T(128)S(1)} %copy-done.5, s32[2,1,2]{2,1,0:T(1,128)S(1)} %copy-done.3, f32[2,256]{1,0:T(2,128)S(1)} %copy-done.2), custom_call_target="tpu_custom_call" | custom-call | tf_op jit(solution)/shard_map/pallas_call | solution.py:321
  42.3 0.0 copy-start.4
  42.3 0.7 %copy-done.4 = f32[2,256]{1,0:T(2,128)S(1)} copy-done((f32[2,256]{1,0:T(2,128)S(1)}, f32[2,256]{1,0:T(2,128)}, u32[]{:S(2)}) %copy-start.4) | copy-done | bytes 2072
  43.0 15.7 %shard_map.65 = f32[128,1024]{1,0:T(8,128)} custom-call(f32[128,1024]{1,0:T(8,128)S(1)} %copy-done, f32[2,4,8,8,1024]{4,3,2,1,0:T(8,128)S(1)} %get-tuple-element.8.g_ref, f32[256,256]{1,0:T(8,128)S(1)} %get-tuple-element.9.inv_ref, f32[4,8,128]{2,1,0:T(8,128)S(1)} %get-tuple-element.10.note_ref, s32[2,256]{1,0:T(2,128)S(1)} %copy-done.1, s32[2]{0:T(128)S(1)} %copy-done.5, ...), custom_call_target="tpu_custom_call" | custom-call | tf_op jit(solution)/shard_map/pallas_call | solution.py:350
Async XLA Ops:
  0.0 1.0 %copy-start = (f32[128,1024]{1,0:T(8,128)S(1)}, f32[128,1024]{1,0:T(8,128)}, u32[]{:S(2)}) copy-start(f32[128,1024]{1,0:T(8,128)} %x_ref.3) | copy-start | bytes 1572868
  1.0 0.7 %copy-start.1 = (s32[2,256]{1,0:T(2,128)S(1)}, s32[2,256]{1,0:T(2,128)}, u32[]{:S(2)}) copy-start(s32[2,256]{1,0:T(2,128)} %rows_ref.3) | copy-start | bytes 6148
  1.7 0.7 %copy-start.2 = (f32[2,256]{1,0:T(2,128)S(1)}, f32[2,256]{1,0:T(2,128)}, u32[]{:S(2)}) copy-start(f32[2,256]{1,0:T(2,128)} %var_ref.3) | copy-start | bytes 6148
  2.4 0.7 %copy-start.3 = (s32[2,1,2]{2,1,0:T(1,128)S(1)}, s32[2,1,2]{2,1,0:T(1,128)}, u32[]{:S(2)}) copy-start(s32[2,1,2]{2,1,0:T(1,128)} %mask_ref.3) | copy-start | bytes 52
  3.1 0.7 %copy-start.5 = (s32[2]{0:T(128)S(1)}, s32[2]{0:T(128)}, u32[]{:S(2)}) copy-start(s32[2]{0:T(128)} %owner_ref.3) | copy-start | bytes 28
  42.3 0.7 %copy-start.4 = (f32[2,256]{1,0:T(2,128)S(1)}, f32[2,256]{1,0:T(2,128)}, u32[]{:S(2)}) copy-start(f32[2,256]{1,0:T(2,128)} %val_ref.1) | copy-start | bytes 6148

commit v2 on v1

--- a/solution.py
+++ b/solution.py
@@ -16,6 +16,7 @@
 MESH = pl.DeviceIdType.MESH
 VMEM = pl.BlockSpec(memory_space=pltpu.VMEM)
 SMEM = pl.BlockSpec(memory_space=pltpu.SMEM)
+HBM = pl.BlockSpec(memory_space=pltpu.HBM)
 
 
 def split2(x):
@@ -38,7 +39,7 @@
     return mm(a[0], b[0], dims) + (mm(a[0], b[1], dims) + mm(a[1], b[0], dims))
 
 
-def sweep_inverse(cov):
+def sweep_inverse(cov, begin=0, end=None):
     size = cov.shape[0]
     lane = lax.broadcasted_iota(jnp.int32, (W, size), 1)
     row = lax.broadcasted_iota(jnp.int32, (W, size), 0)
@@ -75,7 +76,7 @@
         cov[...] = jnp.where(hit, 0.0, cov[...]) - change
         return carry
 
-    lax.fori_loop(0, size // W, body, 0)
+    lax.fori_loop(begin, size // W if end is None else end, body, 0)
 
 
 def row_mean(x):
@@ -90,18 +91,84 @@
     cov[...] = full + jnp.where(r_ids == c_ids, jnp.broadcast_to(var_ref, (size, size)), 0.0)
 
 
-def inverse_of(obs, var_row, cov):
-    covariance(split2(obs - row_mean(obs)), var_row, cov)
-    sweep_inverse(cov)
-
-
-def first_kernel(obs_ref, var_ref, out_ref):
-    inverse_of(obs_ref[...], var_ref[0:1, :], out_ref)
-
-
-def share_kernel(nrows, ncols, x_ref, rows_ref, owner_ref, mask_ref, var_ref, g_ref, note_ref, inv_ref,
-                 src, slots, note_src, note_slots, sum_s, sum_r, line_s, line_r, plane_s, plane_r, pair_s, pair_r,
+def column_of(row, eye):
+    return jnp.sum(jnp.where(eye, jnp.broadcast_to(row, eye.shape), 0.0), axis=1, keepdims=True)
+
+
+def eye_of(count):
+    return (lax.broadcasted_iota(jnp.int32, (count, count), 0)
+            == lax.broadcasted_iota(jnp.int32, (count, count), 1))
+
+
+def widen(values, count):
+    lane = lax.broadcasted_iota(jnp.int32, (1, count), 1)
+    wide = count // len(values)
+    out = jnp.zeros((1, count), F32)
+    for j, value in enumerate(values):
+        out = jnp.where((lane >= j * wide) & (lane < (j + 1) * wide), value, out)
+    return out
+
+
+def taper_of(position, where, mask, local_len):
+    return mask * jnp.exp(-jnp.abs(position - where) / local_len)
+
+
+def my_positions(rows, count, ncols):
+    first = (lax.axis_index("row") * ncols + lax.axis_index("col")) * rows
+    return (first + lax.broadcasted_iota(jnp.int32, (rows, count), 0)).astype(F32)
+
+
+def gain_of(anom2, obs2, neg_inv2, taper, members):
+    cross = dot3(anom2, obs2, NT) * (1.0 / (members - 1.0))
+    return split2(dot3(split2(taper * cross), neg_inv2, NN))
+
+
+def first_batch(nrows, ncols, g_ref, x_ref, rows_ref, owner_ref, mask_ref, val_ref, var_ref,
+                inv_ref, x1_ref, anom_hi, anom_lo, push_hi, push_lo, aux_ref, beside):
+    rows, members = x_ref.shape
+    count = rows_ref.shape[1]
+    nblk = mask_ref.shape[2]
+    local_len = float(rows * nrows * ncols // 4)
+    g0 = g_ref[0].reshape(count, members)
+    m0 = row_mean(g0)
+    a0 = g0 - m0
+    anom_hi[...], anom_lo[...] = split2(a0)
+    covariance((anom_hi[...], anom_lo[...]), var_ref[0:1, :], inv_ref)
+    beside(0)
+    lane = lax.broadcasted_iota(jnp.int32, (1, count), 1)
+    device = jnp.zeros((1, count), jnp.int32)
+    for c in range(1, ncols):
+        device = device + jnp.where(lane >= c * (count // ncols), 1, 0)
+    for b in range(2):
+        aux_ref[b:b + 1, :] = ((owner_ref[b] * ncols + device) * rows + rows_ref[b:b + 1, :]).astype(F32)
+        aux_ref[2 + b:3 + b, :] = widen([mask_ref[b, 0, j].astype(F32) for j in range(nblk)], count)
+    aux_ref[4:6, :] = val_ref[...]
+    aux_ref[6:8, :] = var_ref[...]
+    push_hi[...], push_lo[...] = split2(column_of(val_ref[0:1, :], eye_of(count)) - m0 - 0.5 * a0)
+    mid = 3 * (count // W) // 4
+    sweep_inverse(inv_ref, 0, mid)
+    beside(1)
+    sweep_inverse(inv_ref, mid)
+    x = x_ref[...]
+    taper = taper_of(my_positions(rows, count, ncols), aux_ref[0:1, :], aux_ref[2:3, :], local_len)
+    gain = gain_of(split2(x - row_mean(x)), (anom_hi[...], anom_lo[...]), split2(inv_ref[...]), taper, members)
+    x1_ref[...] = x - dot3(gain, (push_hi[...], push_lo[...]), NN)
+    beside(2)
+
+
+def solo_kernel(nrows, ncols, *refs):
+    first_batch(nrows, ncols, *refs, lambda stage: None)
+
+
+def share_kernel(nrows, ncols, x_hbm, rows_hbm, owner_hbm, mask_hbm, val_hbm, var_hbm, g_ref, note_ref,
+                 inv_ref, x1_ref, anom_hi, anom_lo, push_hi, push_lo, aux_ref,
+                 x_ref, rows_ref, owner_ref, mask_ref, val_ref, var_ref, load, src, slots, note_src, note_slots, sum_s, sum_r, line_s, line_r, plane_s, plane_r, pair_s, pair_r,
                  nsum_s, nsum_r, nline_s, nline_r):
+    loads = [pltpu.make_async_copy(source, target, load.at[k]) for k, (source, target) in enumerate((
+        (x_hbm, x_ref), (rows_hbm, rows_ref), (owner_hbm, owner_ref), (mask_hbm, mask_ref),
+        (val_hbm, val_ref), (var_hbm, var_ref)))]
+    for copy in loads:
+        copy.start()
     me = lax.axis_index("row")
     col = lax.axis_index("col")
     nstate, members = x_ref.shape
@@ -124,6 +191,8 @@
         copy.start()
         return copy
 
+    for copy in loads:
+        copy.wait()
     x3 = split3(x_ref[...])
     state_ids = lax.broadcasted_iota(jnp.int32, (nstate, per_dev), 0)
     sent = []
@@ -176,14 +245,17 @@
         return planes, pairs
 
     def in_chip(b, planes, pairs):
+        hand_on(b, planes, pairs)
+        for copy in pairs:
+            copy.wait_recv()
+
+    def hand_on(b, planes, pairs):
         for d in range(ncols):
             for c in range(1, half):
                 planes[d][c - 1].wait_recv()
                 slab = g_ref.at[b, (col + ncols - d) % ncols, (me + nrows - 2 * c) % nrows]
                 pairs.append(put(slab, slab, pair_s.at[b, d, c], pair_r.at[b, d, c], sibling, col))
                 sent.append(pairs[-1])
-        for copy in pairs:
-            copy.wait_recv()
 
     lane = lax.broadcasted_iota(jnp.int32, (8, 128), 1)
     note = jnp.zeros((8, 128), F32)
@@ -212,80 +284,46 @@
     note_ref[col] = total
     note_lines = [put(note_ref.at[col], note_ref.at[col], nline_s.at[d - 1], nline_r.at[d - 1], me, (col + d) % ncols)
                   for d in range(1, ncols)]
-    obs = g_ref[0].reshape(count, members)
-    covariance(split2(obs - row_mean(obs)), var_ref[0:1, :], inv_ref)
-    planes1, pairs1 = in_plane(1, lines1, first1)
-    sweep_inverse(inv_ref)
-    in_chip(1, planes1, pairs1)
-    for copy in note_lines:
-        copy.wait_recv()
+    later = []
+
+    def beside(stage):
+        if stage == 0:
+            later.extend(in_plane(1, lines1, first1))
+        elif stage == 1:
+            hand_on(1, *later)
+        else:
+            for copy in later[1] + note_lines:
+                copy.wait_recv()
+
+    first_batch(nrows, ncols, g_ref, x_ref, rows_ref, owner_ref, mask_ref, val_ref, var_ref,
+                inv_ref, x1_ref, anom_hi, anom_lo, push_hi, push_lo, aux_ref, beside)
     for copy in sent + notes + note_lines:
         copy.wait_send()
 
 
-def column_of(row, eye):
-    return jnp.sum(jnp.where(eye, jnp.broadcast_to(row, eye.shape), 0.0), axis=1, keepdims=True)
-
-
-def gain_step(anom2, obs2, neg_inv2, taper, members):
-    cross = dot3(anom2, obs2, NT) * (1.0 / (members - 1.0))
-    return dot3(split2(taper * cross), neg_inv2, NN)
-
-
-def second_kernel(nrows, ncols, x_ref, g_ref, inv_ref, note_ref, rows_ref, owner_ref, val_ref, var_ref, mask_ref,
-                  out_ref, x1, g1, cov):
-    rows, members = x_ref.shape
-    count = rows_ref.shape[1]
-    per_dev = count // ncols
-    nblk = mask_ref.shape[2]
-    wide = count // nblk
+def second_kernel(nrows, ncols, nblk, g_ref, note_ref, inv_ref, x1_ref, anom_hi, anom_lo, push_hi, push_lo, aux_ref,
+                  out_ref, g1, cov):
+    rows, members = x1_ref.shape
+    count = inv_ref.shape[0]
     local_len = float(rows * nrows * ncols // 4)
-    eye = (lax.broadcasted_iota(jnp.int32, (count, count), 0)
-           == lax.broadcasted_iota(jnp.int32, (count, count), 1))
-    lane = lax.broadcasted_iota(jnp.int32, (1, count), 1)
-    device = jnp.zeros((1, count), jnp.int32)
-    for c in range(1, ncols):
-        device = device + jnp.where(lane >= c * per_dev, 1, 0)
-    glob = [((owner_ref[b] * ncols + device) * rows + rows_ref[b:b + 1, :]).astype(F32) for b in range(2)]
-    first = (lax.axis_index("row") * ncols + lax.axis_index("col")) * rows
-    pos = (first + lax.broadcasted_iota(jnp.int32, (rows, count), 0)).astype(F32)
-
-    def widen(values):
-        out = jnp.zeros((1, count), F32)
-        for j, value in enumerate(values):
-            out = jnp.where((lane >= j * wide) & (lane < (j + 1) * wide), value, out)
-        return out
-
-    def taper_of(position, where, mask):
-        return mask * jnp.exp(-jnp.abs(position - where) / local_len)
-
-    mask = [widen([mask_ref[b, 0, j].astype(F32) for j in range(nblk)]) for b in range(2)]
+    eye = eye_of(count)
     mask_g = jnp.concatenate(
-        [jnp.broadcast_to(widen([note_ref[c, 0:1, j:j + 1] for j in range(nblk)]), (per_dev, count))
+        [jnp.broadcast_to(widen([note_ref[c, 0:1, j:j + 1] for j in range(nblk)], count), (count // ncols, count))
          for c in range(ncols)], axis=0)
-    gcol = column_of(glob[1], eye)
-
-    g0 = g_ref[0].reshape(count, members)
-    m0 = row_mean(g0)
-    a0 = g0 - m0
-    a02 = split2(a0)
-    inv2 = split2(inv_ref[...])
-    push = split2(column_of(val_ref[0:1, :], eye) - m0 - 0.5 * a0)
-    for src, where, held, dst in ((g_ref[1].reshape(count, members), gcol, mask_g, g1),
-                                  (x_ref[...], pos, mask[0], x1)):
-        taper = taper_of(where, glob[0], held)
-        gain = split2(gain_step(split2(src - row_mean(src)), a02, inv2, taper, members))
-        dst[...] = src - dot3(gain, push, NN)
+    taper = taper_of(column_of(aux_ref[1:2, :], eye), aux_ref[0:1, :], mask_g, local_len)
+    g = g_ref[1].reshape(count, members)
+    gain = gain_of(split2(g - row_mean(g)), (anom_hi[...], anom_lo[...]), split2(inv_ref[...]), taper, members)
+    g1[...] = g - dot3(gain, (push_hi[...], push_lo[...]), NN)
     g = g1[...]
     m1 = row_mean(g)
     a1 = g - m1
     a12 = split2(a1)
-    covariance(a12, var_ref[1:2, :], cov)
+    covariance(a12, aux_ref[7:8, :], cov)
     sweep_inverse(cov)
-    push = split2(column_of(val_ref[1:2, :], eye) - m1 - 0.5 * a1)
-    x = x1[...]
-    taper = taper_of(pos, glob[1], mask[1])
-    gain = split2(gain_step(split2(x - row_mean(x)), a12, split2(cov[...]), taper, members))
+    push = split2(column_of(aux_ref[5:6, :], eye) - m1 - 0.5 * a1)
+    x = x1_ref[...]
+    taper = taper_of(my_positions(rows, count, ncols), aux_ref[1:2, :], aux_ref[3:4, :], local_len)
+    gain = gain_of(split2(x - row_mean(x)), a12, split2(cov[...]), taper, members)
     out_ref[...] = x - dot3(gain, push, NN)
 
 
@@ -313,21 +351,34 @@
     rows, members = ensemble.shape
     batches, count = obs_rows.shape
     per_dev = count // ncols
-    inv_shape = jax.ShapeDtypeStruct((count, count), F32)
+    half_shape = jax.ShapeDtypeStruct((count, members), BF16)
+    kept = (
+        jax.ShapeDtypeStruct((count, count), F32),
+        jax.ShapeDtypeStruct((rows, members), F32),
+        half_shape, half_shape, half_shape, half_shape,
+        jax.ShapeDtypeStruct((8, count), F32),
+    )
+    limit = 40 * 2**20
     if per_dev % (8 * nrows) == 0 and nrows % 2 == 0:
         q = per_dev // nrows
         half = nrows // 2
         dma = pltpu.SemaphoreType.DMA
-        shared, note, inv = pl.pallas_call(
+        shared, note, *held = pl.pallas_call(
             functools.partial(share_kernel, nrows, ncols),
             out_shape=(
                 jax.ShapeDtypeStruct((batches, ncols, nrows, q, members), F32),
                 jax.ShapeDtypeStruct((ncols, 8, 128), F32),
-                inv_shape,
-            ),
-            in_specs=[VMEM, VMEM, SMEM, SMEM, VMEM],
-            out_specs=(VMEM, VMEM, VMEM),
+            ) + kept,
+            in_specs=[HBM] * 6,
+            out_specs=(VMEM,) * 9,
             scratch_shapes=[
+                pltpu.VMEM(ensemble.shape, F32),
+                pltpu.VMEM(obs_rows.shape, jnp.int32),
+                pltpu.SMEM(owner.shape, jnp.int32),
+                pltpu.SMEM(taper_mask.shape, jnp.int32),
+                pltpu.VMEM(obs_value.shape, F32),
+                pltpu.VMEM(obs_var.shape, F32),
+                dma((6,)),
                 pltpu.VMEM((batches, per_dev, members), F32),
                 pltpu.VMEM((batches, nrows - 1, q, members), F32),
                 pltpu.VMEM((8, 128), F32),
@@ -336,29 +387,26 @@
             + [dma((batches, ncols, half - 1))] * 2 + [dma((batches, ncols, half))] * 2
             + [dma((nrows - 1,))] * 2 + [dma((ncols - 1,))] * 2,
             compiler_params=pltpu.CompilerParams(
-                vmem_limit_bytes=40 * 2**20, collective_id=0, has_side_effects=True),
-        )(ensemble, obs_rows, owner, taper_mask, obs_var)
+                vmem_limit_bytes=limit, collective_id=0, has_side_effects=True),
+        )(*[pltpu.with_memory_space_constraint(arg, pltpu.HBM)
+            for arg in (ensemble, obs_rows, owner, taper_mask, obs_value, obs_var)])
     else:
         shared, note = shared_by_collectives(ensemble, obs_rows, owner, taper_mask, ncols)
-        inv = pl.pallas_call(
-            first_kernel,
-            out_shape=inv_shape,
-            in_specs=[VMEM] * 2,
-            out_specs=VMEM,
-            compiler_params=pltpu.CompilerParams(vmem_limit_bytes=40 * 2**20),
-        )(shared[0], obs_var)
+        held = pl.pallas_call(
+            functools.partial(solo_kernel, nrows, ncols),
+            out_shape=kept,
+            in_specs=[VMEM] * 3 + [SMEM] * 2 + [VMEM] * 2,
+            out_specs=(VMEM,) * 7,
+            compiler_params=pltpu.CompilerParams(vmem_limit_bytes=limit),
+        )(shared, ensemble, obs_rows, owner, taper_mask, obs_value, obs_var)
     return pl.pallas_call(
-        functools.partial(second_kernel, nrows, ncols),
+        functools.partial(second_kernel, nrows, ncols, taper_mask.shape[2]),
         out_shape=jax.ShapeDtypeStruct((rows, members), F32),
-        in_specs=[VMEM] * 5 + [SMEM, VMEM, VMEM, SMEM],
+        in_specs=[VMEM] * 9,
         out_specs=VMEM,
-        scratch_shapes=[
-            pltpu.VMEM((rows, members), F32),
-            pltpu.VMEM((count, members), F32),
-            pltpu.VMEM((count, count), F32),
-        ],
-        compiler_params=pltpu.CompilerParams(vmem_limit_bytes=40 * 2**20),
-    )(ensemble, shared, inv, note, obs_rows, owner, obs_value, obs_var, taper_mask)
+        scratch_shapes=[pltpu.VMEM((count, members), F32), pltpu.VMEM((count, count), F32)],
+        compiler_params=pltpu.CompilerParams(vmem_limit_bytes=limit),
+    )(shared, note, *held)
 
 
 def solution(mesh):

time: 59 us -> 53 us (0.90)
  local copies, waits for them, and re-layouts: 4.41 us -> 0 us
  Pallas kernels: 54.3 us -> 52.8 us
    unnamed x12 -> x0, local copies, waits for them, and re-layouts: 4.41 us -> none
    pallas_call x1, Pallas kernels: 15.7 us -> 14.1 us  [on_device(): pl.pallas_call(functools.partial(second_kernel, nrows, ncols, taper_mask....]
where the time goes in v2:
time: 53 us; the launch traced here: 52.8 us
  Pallas kernels  52.8 us (100%)
    pallas_call x1, Pallas kernels, on_device(): pl.pallas_call(functools.partial(share_kernel, nrows, ncols), out_shape=(...  38.7 us
    pallas_call x1, Pallas kernels, on_device(): pl.pallas_call(functools.partial(second_kernel, nrows, ncols, taper_mask....  14.1 us

profile of v2, /device:TPU:0, one launch (start us, length us, event | category | flops | bytes accessed | tf_op | source)
XLA Modules:
  0.0 52.8 jit_solution(4717335709916894849)
XLA Ops:
  0.0 38.7 %shard_map.64 = (f32[2,4,8,8,1024]{4,3,2,1,0:T(8,128)S(1)}, f32[4,8,128]{2,1,0:T(8,128)S(1)}, f32[256,256]{1,0:T(8,128)S(1)}, f32[128,1024]{1,0:T(8,128)S(1)}, b...) custom-call(f32[128,1024]{1,0:T(8,128)} %x_hbm.1, ...), custom_call_target="tpu_custom_call" | custom-call | tf_op jit(solution)/shard_map/pallas_call | solution.py:366
  38.7 14.1 %shard_map.65 = f32[128,1024]{1,0:T(8,128)} custom-call(f32[2,4,8,8,1024]{4,3,2,1,0:T(8,128)S(1)} %get-tuple-element.14.g_ref, f32[4,8,128]{2,1,0:T(8,128)S(1)} %get-tuple-element.15.note_ref, f32[256,256]{1,0:T(8,128)S(1)} %get-tuple-element.16.inv_ref, f32[128,1024]{1,0:T(8,128)S(1)} %get-tuple-element.17.x1_ref, ...), custom_call_target="tpu_custom_call" | custom-call | tf_op jit(solution)/shard_map/pallas_call | solution.py:402

commit v3 on v2

--- a/solution.py
+++ b/solution.py
@@ -145,24 +145,35 @@
     aux_ref[4:6, :] = val_ref[...]
     aux_ref[6:8, :] = var_ref[...]
     push_hi[...], push_lo[...] = split2(column_of(val_ref[0:1, :], eye_of(count)) - m0 - 0.5 * a0)
-    mid = 3 * (count // W) // 4
-    sweep_inverse(inv_ref, 0, mid)
-    beside(1)
-    sweep_inverse(inv_ref, mid)
+    steps = count // W
+    cuts = [0, steps // 4, steps // 2, 13 * steps // 16, steps]
+    for k in range(4):
+        sweep_inverse(inv_ref, cuts[k], cuts[k + 1])
+        beside(k + 1)
     x = x_ref[...]
     taper = taper_of(my_positions(rows, count, ncols), aux_ref[0:1, :], aux_ref[2:3, :], local_len)
     gain = gain_of(split2(x - row_mean(x)), (anom_hi[...], anom_lo[...]), split2(inv_ref[...]), taper, members)
     x1_ref[...] = x - dot3(gain, (push_hi[...], push_lo[...]), NN)
-    beside(2)
+    beside(5)
 
 
 def solo_kernel(nrows, ncols, *refs):
     first_batch(nrows, ncols, *refs, lambda stage: None)
 
 
+def flip(index, bits):
+    bit = 1
+    while bit <= bits:
+        if bits & bit:
+            index = index + bit - 2 * bit * ((index // bit) % 2)
+        bit *= 2
+    return index
+
+
 def share_kernel(nrows, ncols, x_hbm, rows_hbm, owner_hbm, mask_hbm, val_hbm, var_hbm, g_ref, note_ref,
                  inv_ref, x1_ref, anom_hi, anom_lo, push_hi, push_lo, aux_ref,
-                 x_ref, rows_ref, owner_ref, mask_ref, val_ref, var_ref, load, src, slots, note_src, note_slots, sum_s, sum_r, line_s, line_r, plane_s, plane_r, pair_s, pair_r,
+                 x_ref, rows_ref, owner_ref, mask_ref, val_ref, var_ref, load, src, core_slot, part, slots,
+                 note_src, note_slots, core_s, core_r, sum_s, sum_r, line_s, line_r, plane_s, plane_r, pair_s, pair_r,
                  nsum_s, nsum_r, nline_s, nline_r):
     loads = [pltpu.make_async_copy(source, target, load.at[k]) for k, (source, target) in enumerate((
         (x_hbm, x_ref), (rows_hbm, rows_ref), (owner_hbm, owner_ref), (mask_hbm, mask_ref),
@@ -176,26 +187,37 @@
     per_dev = count // ncols
     q = per_dev // nrows
     half = nrows // 2
-    sibling = me + 1 - 2 * (me % 2)
+    core = me % 2
+    chip = me // 2
+    sibling = flip(me, 1)
+    beside_x = flip(me, 2)
+    beside_y = flip(me, 4)
+    across = flip(me, 6)
+    cut = members // 2
 
     barrier = pltpu.get_barrier_semaphore()
     for d in range(1, nrows):
-        pl.semaphore_signal(barrier, inc=1, device_id=((me + d) % nrows, col), device_id_type=MESH)
+        pl.semaphore_signal(barrier, inc=1, device_id=(flip(me, d), col), device_id_type=MESH)
     for d in range(1, ncols):
-        pl.semaphore_signal(barrier, inc=1, device_id=(me, (col + d) % ncols), device_id_type=MESH)
+        pl.semaphore_signal(barrier, inc=1, device_id=(me, flip(col, d)), device_id_type=MESH)
+
+    sent = []
 
     def put(source, target, send, recv, row, column):
         copy = pltpu.make_async_remote_copy(
             src_ref=source, dst_ref=target, send_sem=send, recv_sem=recv,
             device_id=(row, column), device_id_type=MESH)
         copy.start()
+        sent.append(copy)
         return copy
+
+    def same(ref, send, recv, row):
+        return put(ref, ref, send, recv, row, col)
 
     for copy in loads:
         copy.wait()
     x3 = split3(x_ref[...])
     state_ids = lax.broadcasted_iota(jnp.int32, (nstate, per_dev), 0)
-    sent = []
 
     def select(b):
         ids = jnp.broadcast_to(rows_ref[b:b + 1, :], (8, count))
@@ -203,39 +225,36 @@
         here = jnp.full((1, per_dev), owner_ref[b], jnp.int32) == me
         ids = jnp.where(here, ids, -1)
         pick = jnp.where(ids == state_ids, 1.0, 0.0).astype(BF16)
-        src[b] = (mm(pick, x3[0], TN) + mm(pick, x3[1], TN)) + mm(pick, x3[2], TN)
-
-    def scatter(b):
-        copies = []
-        for d in range(1, nrows):
-            peer = (me + d) % nrows
-            copies.append(put(src.at[b, pl.ds(pl.multiple_of(peer * q, q), q)], slots.at[b, d - 1],
-                              sum_s.at[b, d - 1], sum_r.at[b, d - 1], peer, col))
-        sent.extend(copies)
-        return copies
+        rows = (mm(pick, x3[0], TN) + mm(pick, x3[1], TN)) + mm(pick, x3[2], TN)
+        src[b] = rows.reshape(half, 2, q, members)
+
+    def to_core(b):
+        return put(src.at[b, :, 1 - core], core_slot.at[b], core_s.at[b], core_r.at[b], sibling, col)
+
+    def to_chips(b, copy):
+        copy.wait_recv()
+        part[b] = src[b, :, core] + core_slot[b]
+        return [put(part.at[b, flip(chip, d)], slots.at[b, d - 1], sum_s.at[b, d - 1], sum_r.at[b, d - 1],
+                    flip(me, 2 * d), col) for d in range(1, half)]
 
     def along_line(b, copies):
         for copy in copies:
             copy.wait_recv()
-        total = src[b, pl.ds(pl.multiple_of(me * q, q), q), :]
-        for d in range(1, nrows):
+        total = part[b, chip]
+        for d in range(1, half):
             total = total + slots[b, d - 1]
         g_ref[b, col, me] = total
         mine = g_ref.at[b, col, me]
-        copies = [put(mine, mine, line_s.at[b, d - 1], line_r.at[b, d - 1], me, (col + d) % ncols)
-                  for d in range(1, ncols)]
-        sent.extend(copies)
-        return copies
+        return [put(mine, mine, line_s.at[b, d - 1], line_r.at[b, d - 1], me, flip(col, d))
+                for d in range(1, ncols)]
 
     def spread(b, d):
-        slab = g_ref.at[b, (col + ncols - d) % ncols, me]
-        copies = [put(slab, slab, plane_s.at[b, d, c - 1], plane_r.at[b, d, c - 1], (me + 2 * c) % nrows, col)
-                  for c in range(1, half)]
-        pairs = [put(slab, slab, pair_s.at[b, d, 0], pair_r.at[b, d, 0], sibling, col)]
-        sent.extend(copies + pairs)
-        return copies, pairs
-
-    def in_plane(b, lines, first):
+        slab = g_ref.at[b, flip(col, d), me]
+        x_copy = same(slab, plane_s.at[b, d, 0], plane_r.at[b, d, 0], beside_x)
+        y_copy = same(slab, plane_s.at[b, d, 1], plane_r.at[b, d, 1], beside_y)
+        return [x_copy, y_copy], [same(slab, pair_s.at[b, d, 0], pair_r.at[b, d, 0], sibling)]
+
+    def spread_lines(b, lines, first):
         planes, pairs = [first[0]], list(first[1])
         for d in range(1, ncols):
             lines[d - 1].wait_recv()
@@ -244,18 +263,25 @@
             pairs.extend(more[1])
         return planes, pairs
 
-    def in_chip(b, planes, pairs):
-        hand_on(b, planes, pairs)
-        for copy in pairs:
-            copy.wait_recv()
-
-    def hand_on(b, planes, pairs):
+    def relay(b, d, planes, pairs):
+        planes[d][0].wait_recv()
+        slab = g_ref.at[b, flip(col, d), beside_x]
+        planes[d].append(same(slab.at[:, :cut], plane_s.at[b, d, 2], plane_r.at[b, d, 2], beside_y))
+        pairs.append(same(slab, pair_s.at[b, d, 1], pair_r.at[b, d, 1], sibling))
+        planes[d][1].wait_recv()
+        slab = g_ref.at[b, flip(col, d), beside_y]
+        planes[d].append(same(slab.at[:, cut:], plane_s.at[b, d, 3], plane_r.at[b, d, 3], beside_x))
+        pairs.append(same(slab, pair_s.at[b, d, 2], pair_r.at[b, d, 2], sibling))
+
+    def relay_all(b, planes, pairs):
         for d in range(ncols):
-            for c in range(1, half):
-                planes[d][c - 1].wait_recv()
-                slab = g_ref.at[b, (col + ncols - d) % ncols, (me + nrows - 2 * c) % nrows]
-                pairs.append(put(slab, slab, pair_s.at[b, d, c], pair_r.at[b, d, c], sibling, col))
-                sent.append(pairs[-1])
+            relay(b, d, planes, pairs)
+
+    def finish(b, planes, pairs):
+        for d in range(ncols):
+            planes[d][2].wait_recv()
+            planes[d][3].wait_recv()
+            pairs.append(same(g_ref.at[b, flip(col, d), across], pair_s.at[b, d, 3], pair_r.at[b, d, 3], sibling))
 
     lane = lax.broadcasted_iota(jnp.int32, (8, 128), 1)
     note = jnp.zeros((8, 128), F32)
@@ -265,39 +291,46 @@
     note_src[...] = jnp.where(here, note, 0.0)
     select(0)
     pl.semaphore_wait(barrier, nrows + ncols - 2)
-    sums0 = scatter(0)
+    core0 = to_core(0)
     select(1)
+    sums0 = to_chips(0, core0)
+    core1 = to_core(1)
     lines0 = along_line(0, sums0)
     first0 = spread(0, 0)
-    notes = [put(note_src, note_slots.at[d - 1], nsum_s.at[d - 1], nsum_r.at[d - 1], (me + d) % nrows, col)
+    notes = [put(note_src, note_slots.at[d - 1], nsum_s.at[d - 1], nsum_r.at[d - 1], flip(me, d), col)
              for d in range(1, nrows)]
-    planes0, pairs0 = in_plane(0, lines0, first0)
-    sums1 = scatter(1)
-    in_chip(0, planes0, pairs0)
-
-    lines1 = along_line(1, sums1)
-    first1 = spread(1, 0)
+    planes0, pairs0 = spread_lines(0, lines0, first0)
+    relay_all(0, planes0, pairs0)
+    sums1 = to_chips(1, core1)
+    finish(0, planes0, pairs0)
     total = note_src[...]
     for d in range(1, nrows):
         notes[d - 1].wait_recv()
         total = total + note_slots[d - 1]
     note_ref[col] = total
-    note_lines = [put(note_ref.at[col], note_ref.at[col], nline_s.at[d - 1], nline_r.at[d - 1], me, (col + d) % ncols)
+    note_lines = [put(note_ref.at[col], note_ref.at[col], nline_s.at[d - 1], nline_r.at[d - 1], me, flip(col, d))
                   for d in range(1, ncols)]
+    for copy in pairs0:
+        copy.wait_recv()
     later = []
 
     def beside(stage):
         if stage == 0:
-            later.extend(in_plane(1, lines1, first1))
+            lines1 = along_line(1, sums1)
+            later.extend([lines1, spread(1, 0)])
         elif stage == 1:
-            hand_on(1, *later)
-        else:
+            later[:] = spread_lines(1, *later)
+        elif stage == 2:
+            relay_all(1, *later)
+        elif stage == 3:
+            finish(1, *later)
+        elif stage == 5:
             for copy in later[1] + note_lines:
                 copy.wait_recv()
 
     first_batch(nrows, ncols, g_ref, x_ref, rows_ref, owner_ref, mask_ref, val_ref, var_ref,
                 inv_ref, x1_ref, anom_hi, anom_lo, push_hi, push_lo, aux_ref, beside)
-    for copy in sent + notes + note_lines:
+    for copy in sent:
         copy.wait_send()
 
 
@@ -359,7 +392,7 @@
         jax.ShapeDtypeStruct((8, count), F32),
     )
     limit = 40 * 2**20
-    if per_dev % (8 * nrows) == 0 and nrows % 2 == 0:
+    if nrows == 8 and ncols & (ncols - 1) == 0 and per_dev % (8 * nrows) == 0:
         q = per_dev // nrows
         half = nrows // 2
         dma = pltpu.SemaphoreType.DMA
@@ -379,13 +412,14 @@
                 pltpu.VMEM(obs_value.shape, F32),
                 pltpu.VMEM(obs_var.shape, F32),
                 dma((6,)),
-                pltpu.VMEM((batches, per_dev, members), F32),
-                pltpu.VMEM((batches, nrows - 1, q, members), F32),
+                pltpu.VMEM((batches, half, 2, q, members), F32),
+                pltpu.VMEM((batches, half, q, members), F32),
+                pltpu.VMEM((batches, half, q, members), F32),
+                pltpu.VMEM((batches, half - 1, q, members), F32),
                 pltpu.VMEM((8, 128), F32),
                 pltpu.VMEM((nrows - 1, 8, 128), F32),
-            ] + [dma((batches, nrows - 1))] * 2 + [dma((batches, ncols - 1))] * 2
-            + [dma((batches, ncols, half - 1))] * 2 + [dma((batches, ncols, half))] * 2
-            + [dma((nrows - 1,))] * 2 + [dma((ncols - 1,))] * 2,
+            ] + [dma((batches,))] * 2 + [dma((batches, half - 1))] * 2 + [dma((batches, ncols - 1))] * 2
+            + [dma((batches, ncols, 4))] * 4 + [dma((nrows - 1,))] * 2 + [dma((ncols - 1,))] * 2,
             compiler_params=pltpu.CompilerParams(
                 vmem_limit_bytes=limit, collective_id=0, has_side_effects=True),
         )(*[pltpu.with_memory_space_constraint(arg, pltpu.HBM)

time: 53 us -> 52.8 us (level)
  no operation moved by 1% of the time
where the time goes in v3:
time: 52.8 us; the launch traced here: 52.7 us
  Pallas kernels  52.7 us (100%)
    pallas_call x1, Pallas kernels, on_device(): pl.pallas_call(functools.partial(share_kernel, nrows, ncols), out_shape=(...  38.6 us
    pallas_call x1, Pallas kernels, on_device(): pl.pallas_call(functools.partial(second_kernel, nrows, ncols, taper_mask....  14.1 us

profile of v3, /device:TPU:0, one launch (start us, length us, event | category | flops | bytes accessed | tf_op | source)
XLA Modules:
  0.0 52.7 jit_solution(14280483581610123438)
XLA Ops:
  0.0 38.6 %shard_map.64 = (f32[2,4,8,8,1024]{4,3,2,1,0:T(8,128)S(1)}, f32[4,8,128]{2,1,0:T(8,128)S(1)}, f32[256,256]{1,0:T(8,128)S(1)}, f32[128,1024]{1,0:T(8,128)S(1)}, b...) custom-call(f32[128,1024]{1,0:T(8,128)} %x_hbm.1, ...), custom_call_target="tpu_custom_call" | custom-call | tf_op jit(solution)/shard_map/pallas_call | solution.py:399
  38.6 14.1 %shard_map.65 = f32[128,1024]{1,0:T(8,128)} custom-call(f32[2,4,8,8,1024]{4,3,2,1,0:T(8,128)S(1)} %get-tuple-element.14.g_ref, f32[4,8,128]{2,1,0:T(8,128)S(1)} %get-tuple-element.15.note_ref, f32[256,256]{1,0:T(8,128)S(1)} %get-tuple-element.16.inv_ref, f32[128,1024]{1,0:T(8,128)S(1)} %get-tuple-element.17.x1_ref, ...), custom_call_target="tpu_custom_call" | custom-call | tf_op jit(solution)/shard_map/pallas_call | solution.py:436

commit v4 on v3

--- a/solution.py
+++ b/solution.py
@@ -39,44 +39,78 @@
     return mm(a[0], b[0], dims) + (mm(a[0], b[1], dims) + mm(a[1], b[0], dims))
 
 
-def sweep_inverse(cov, begin=0, end=None):
+def eliminate(cols, right):
+    size = right.shape[1]
+    row = lax.broadcasted_iota(jnp.int32, (W, 128), 0)
+    same = jnp.zeros((W, 128), F32)
+    other = jnp.zeros((W, 128), F32)
+    widen_lanes = lambda v: jnp.concatenate([v] * (size // 128), axis=1)
+    for j in range(0, W, 2):
+        a, b, d = cols[j][j:j + 1, :], cols[j + 1][j:j + 1, :], cols[j + 1][j + 1:j + 2, :]
+        det = a * d - b * b
+        r = pl.reciprocal(det, approx=True)
+        r = r * (2.0 - det * r)
+        r = r * (2.0 - det * r)
+        ar, br, dr = a * r, b * r, d * r
+        pair = (row == j) | (row == j + 1)
+        m1 = jnp.where(pair, 0.0, cols[j])
+        m2 = jnp.where(pair, 0.0, cols[j + 1])
+        same = jnp.where(row == j, dr, jnp.where(row == j + 1, ar, same))
+        other = jnp.where(pair, br, other)
+        for i in range(j + 2, W):
+            x, y = cols[i][j:j + 1, :], cols[i][j + 1:j + 2, :]
+            cols[i] = cols[i] - m1 * (dr * x - br * y) - m2 * (ar * y - br * x)
+        x, y = right[j:j + 1, :], right[j + 1:j + 2, :]
+        arw, brw, drw = widen_lanes(ar), widen_lanes(br), widen_lanes(dr)
+        right = right - widen_lanes(m1) * (drw * x - brw * y) - widen_lanes(m2) * (arw * y - brw * x)
+    even = lax.broadcasted_iota(jnp.int32, (W, size), 0) % 2 == 0
+    swapped = jnp.where(even, pltpu.roll(right, W - 1, 0), pltpu.roll(right, 1, 0))
+    return right * widen_lanes(same) - swapped * widen_lanes(other)
+
+
+def six_terms(left, right):
+    a1, a2, a3 = split3(left)
+    b1, b2, b3 = split3(right)
+    return (jnp.concatenate([a1, a1, a2, a1, a2, a3], axis=0), jnp.concatenate([b1, b2, b1, b3, b2, b1], axis=0))
+
+
+def sweep_apply(cov, lhs, rhs, start):
+    lane = lax.broadcasted_iota(jnp.int32, (1, cov.shape[1]), 1)
+    inside = (lane >= start) & (lane < start + W)
+    cov[...] = jnp.where(inside, 0.0, cov[...]) - mm(lhs[...], rhs[...], TN)
+
+
+def sweep_begin(cov, lhs, rhs):
+    lhs[...] = jnp.zeros(lhs.shape, BF16)
+    rhs[...] = jnp.zeros(rhs.shape, BF16)
+    return cov[0:W, :]
+
+
+def sweep_steps(cov, lhs, rhs, panel, begin, end):
     size = cov.shape[0]
     lane = lax.broadcasted_iota(jnp.int32, (W, size), 1)
     row = lax.broadcasted_iota(jnp.int32, (W, size), 0)
-    row_small = lax.broadcasted_iota(jnp.int32, (W, 128), 0)
-
-    def body(k, carry):
+
+    def body(k, panel):
         start = pl.multiple_of(k * W, W)
-        panel = cov[pl.ds(start, W), :]
+        sweep_apply(cov, lhs, rhs, start - W)
+        cov[pl.ds(start, W), :] = jnp.zeros((W, size), F32)
         rolled = pltpu.roll(panel, size - start, 1)
         cols = [jnp.broadcast_to(rolled[:, i:i + 1], (W, 128)) for i in range(W)]
         inside = (lane >= start) & (lane < start + W)
         left = jnp.where(inside, jnp.where(lane - start == row, -1.0, 0.0), panel)
-        right = left
-        scale = jnp.zeros((W, 128), F32)
-        for j in range(W):
-            inv = 1.0 / cols[j][j:j + 1, :]
-            here = row_small == j
-            mult = jnp.where(here, 0.0, cols[j])
-            scale = jnp.where(here, inv, scale)
-            for i in range(j + 1, W):
-                cols[i] = cols[i] - mult * (cols[i][j:j + 1, :] * inv)
-            wide = jnp.concatenate([mult] * (size // 128), axis=1)
-            wide_inv = jnp.concatenate([inv] * (size // 128), axis=1)
-            right = right - wide * (right[j:j + 1, :] * wide_inv)
-        right = right * jnp.concatenate([scale] * (size // 128), axis=1)
-        a1, a2, a3 = split3(left)
-        b1, b2, b3 = split3(right)
-        lhs = jnp.concatenate([a1, a1, a2, a1, a2, a3], axis=0)
-        rhs = jnp.concatenate([b1, b2, b1, b3, b2, b1], axis=0)
-        change = mm(lhs, rhs, TN)
-        r_ids = lax.broadcasted_iota(jnp.int32, (size, size), 0)
-        c_ids = lax.broadcasted_iota(jnp.int32, (size, size), 1)
-        hit = ((r_ids >= start) & (r_ids < start + W)) | ((c_ids >= start) & (c_ids < start + W))
-        cov[...] = jnp.where(hit, 0.0, cov[...]) - change
-        return carry
-
-    lax.fori_loop(begin, size // W if end is None else end, body, 0)
+        right = eliminate(cols, left)
+        after = ((k + 1) % (size // W)) * W
+        lhs[...], rhs[...] = six_terms(left, right)
+        ahead, _ = six_terms(pltpu.roll(left, size - after, 1)[:, :128], left)
+        coming = jnp.where(inside, 0.0, cov[pl.ds(pl.multiple_of(after, W), W), :])
+        return coming - mm(ahead, rhs[...], TN)[:W, :]
+
+    return lax.fori_loop(begin, end, body, panel)
+
+
+def sweep_end(cov, lhs, rhs):
+    sweep_apply(cov, lhs, rhs, cov.shape[0] - W)
 
 
 def row_mean(x):
@@ -124,7 +158,7 @@
 
 
 def first_batch(nrows, ncols, g_ref, x_ref, rows_ref, owner_ref, mask_ref, val_ref, var_ref,
-                inv_ref, x1_ref, anom_hi, anom_lo, push_hi, push_lo, aux_ref, beside):
+                inv_ref, x1_ref, anom_hi, anom_lo, push_hi, push_lo, aux_ref, lhs, rhs, beside):
     rows, members = x_ref.shape
     count = rows_ref.shape[1]
     nblk = mask_ref.shape[2]
@@ -147,9 +181,11 @@
     push_hi[...], push_lo[...] = split2(column_of(val_ref[0:1, :], eye_of(count)) - m0 - 0.5 * a0)
     steps = count // W
     cuts = [0, steps // 4, steps // 2, 13 * steps // 16, steps]
+    panel = sweep_begin(inv_ref, lhs, rhs)
     for k in range(4):
-        sweep_inverse(inv_ref, cuts[k], cuts[k + 1])
+        panel = sweep_steps(inv_ref, lhs, rhs, panel, cuts[k], cuts[k + 1])
         beside(k + 1)
+    sweep_end(inv_ref, lhs, rhs)
     x = x_ref[...]
     taper = taper_of(my_positions(rows, count, ncols), aux_ref[0:1, :], aux_ref[2:3, :], local_len)
     gain = gain_of(split2(x - row_mean(x)), (anom_hi[...], anom_lo[...]), split2(inv_ref[...]), taper, members)
@@ -172,7 +208,7 @@
 
 def share_kernel(nrows, ncols, x_hbm, rows_hbm, owner_hbm, mask_hbm, val_hbm, var_hbm, g_ref, note_ref,
                  inv_ref, x1_ref, anom_hi, anom_lo, push_hi, push_lo, aux_ref,
-                 x_ref, rows_ref, owner_ref, mask_ref, val_ref, var_ref, load, src, core_slot, part, slots,
+                 lhs, rhs, x_ref, rows_ref, owner_ref, mask_ref, val_ref, var_ref, load, src, core_slot, part, slots,
                  note_src, note_slots, core_s, core_r, sum_s, sum_r, line_s, line_r, plane_s, plane_r, pair_s, pair_r,
                  nsum_s, nsum_r, nline_s, nline_r):
     loads = [pltpu.make_async_copy(source, target, load.at[k]) for k, (source, target) in enumerate((
@@ -329,13 +365,13 @@
                 copy.wait_recv()
 
     first_batch(nrows, ncols, g_ref, x_ref, rows_ref, owner_ref, mask_ref, val_ref, var_ref,
-                inv_ref, x1_ref, anom_hi, anom_lo, push_hi, push_lo, aux_ref, beside)
+                inv_ref, x1_ref, anom_hi, anom_lo, push_hi, push_lo, aux_ref, lhs, rhs, beside)
     for copy in sent:
         copy.wait_send()
 
 
 def second_kernel(nrows, ncols, nblk, g_ref, note_ref, inv_ref, x1_ref, anom_hi, anom_lo, push_hi, push_lo, aux_ref,
-                  out_ref, g1, cov):
+                  out_ref, g1, cov, lhs, rhs):
     rows, members = x1_ref.shape
     count = inv_ref.shape[0]
     local_len = float(rows * nrows * ncols // 4)
@@ -352,7 +388,9 @@
     a1 = g - m1
     a12 = split2(a1)
     covariance(a12, aux_ref[7:8, :], cov)
-    sweep_inverse(cov)
+    panel = sweep_begin(cov, lhs, rhs)
+    sweep_steps(cov, lhs, rhs, panel, 0, count // W)
+    sweep_end(cov, lhs, rhs)
     push = split2(column_of(aux_ref[5:6, :], eye) - m1 - 0.5 * a1)
     x = x1_ref[...]
     taper = taper_of(my_positions(rows, count, ncols), aux_ref[1:2, :], aux_ref[3:4, :], local_len)
@@ -392,6 +430,7 @@
         jax.ShapeDtypeStruct((8, count), F32),
     )
     limit = 40 * 2**20
+    terms = [pltpu.VMEM((6 * W, count), BF16)] * 2
     if nrows == 8 and ncols & (ncols - 1) == 0 and per_dev % (8 * nrows) == 0:
         q = per_dev // nrows
         half = nrows // 2
@@ -404,7 +443,7 @@
             ) + kept,
             in_specs=[HBM] * 6,
             out_specs=(VMEM,) * 9,
-            scratch_shapes=[
+            scratch_shapes=terms + [
                 pltpu.VMEM(ensemble.shape, F32),
                 pltpu.VMEM(obs_rows.shape, jnp.int32),
                 pltpu.SMEM(owner.shape, jnp.int32),
@@ -431,6 +470,7 @@
             out_shape=kept,
             in_specs=[VMEM] * 3 + [SMEM] * 2 + [VMEM] * 2,
             out_specs=(VMEM,) * 7,
+            scratch_shapes=terms,
             compiler_params=pltpu.CompilerParams(vmem_limit_bytes=limit),
         )(shared, ensemble, obs_rows, owner, taper_mask, obs_value, obs_var)
     return pl.pallas_call(
@@ -438,7 +478,7 @@
         out_shape=jax.ShapeDtypeStruct((rows, members), F32),
         in_specs=[VMEM] * 9,
         out_specs=VMEM,
-        scratch_shapes=[pltpu.VMEM((count, members), F32), pltpu.VMEM((count, count), F32)],
+        scratch_shapes=[pltpu.VMEM((count, members), F32), pltpu.VMEM((count, count), F32)] + terms,
         compiler_params=pltpu.CompilerParams(vmem_limit_bytes=limit),
     )(shared, note, *held)
 

time: 52.8 us -> 53.4 us (1.011)
  no operation moved by 1% of the time
where the time goes in v4:
time: 53.4 us; the launch traced here: 53.2 us
  Pallas kernels  53.2 us (100%)
    pallas_call x1, Pallas kernels, on_device(): pl.pallas_call(functools.partial(share_kernel, nrows, ncols), out_shape=(...  38.8 us
    pallas_call x1, Pallas kernels, on_device(): pl.pallas_call(functools.partial(second_kernel, nrows, ncols, taper_mask....  14.4 us

profile of v4, /device:TPU:0, one launch (start us, length us, event | category | flops | bytes accessed | tf_op | source)
XLA Modules:
  0.0 53.2 jit_solution(18067183299093582743)
XLA Ops:
  0.0 38.8 %shard_map.64 = (f32[2,4,8,8,1024]{4,3,2,1,0:T(8,128)S(1)}, f32[4,8,128]{2,1,0:T(8,128)S(1)}, f32[256,256]{1,0:T(8,128)S(1)}, f32[128,1024]{1,0:T(8,128)S(1)}, b...) custom-call(f32[128,1024]{1,0:T(8,128)} %x_hbm.1, ...), custom_call_target="tpu_custom_call" | custom-call | tf_op jit(solution)/shard_map/pallas_call | solution.py:438
  38.8 14.4 %shard_map.65 = f32[128,1024]{1,0:T(8,128)} custom-call(f32[2,4,8,8,1024]{4,3,2,1,0:T(8,128)S(1)} %get-tuple-element.14.g_ref, f32[4,8,128]{2,1,0:T(8,128)S(1)} %get-tuple-element.15.note_ref, f32[256,256]{1,0:T(8,128)S(1)} %get-tuple-element.16.inv_ref, f32[128,1024]{1,0:T(8,128)S(1)} %get-tuple-element.17.x1_ref, ...), custom_call_target="tpu_custom_call" | custom-call | tf_op jit(solution)/shard_map/pallas_call | solution.py:476

commit v5 on v4

--- a/solution.py
+++ b/solution.py
@@ -39,33 +39,42 @@
     return mm(a[0], b[0], dims) + (mm(a[0], b[1], dims) + mm(a[1], b[0], dims))
 
 
-def eliminate(cols, right):
+def eliminate(panel, right):
     size = right.shape[1]
-    row = lax.broadcasted_iota(jnp.int32, (W, 128), 0)
-    same = jnp.zeros((W, 128), F32)
-    other = jnp.zeros((W, 128), F32)
-    widen_lanes = lambda v: jnp.concatenate([v] * (size // 128), axis=1)
+    tiles = range(W // 8)
+    row = lax.broadcasted_iota(jnp.int32, (8, 128), 0)
+    cols = [[jnp.broadcast_to(panel[8 * t:8 * t + 8, i:i + 1], (8, 128)) for t in tiles] for i in range(W)]
+    right = [[right[8 * t:8 * t + 8, h * 128:h * 128 + 128] for t in tiles] for h in range(size // 128)]
+    same = [jnp.zeros((8, 128), F32) for t in tiles]
+    other = [jnp.zeros((8, 128), F32) for t in tiles]
     for j in range(0, W, 2):
-        a, b, d = cols[j][j:j + 1, :], cols[j + 1][j:j + 1, :], cols[j + 1][j + 1:j + 2, :]
+        home, at = j // 8, j % 8
+        take = lambda v, k: jnp.broadcast_to(v[home][k:k + 1, :], (8, 128))
+        a, b, d = take(cols[j], at), take(cols[j + 1], at), take(cols[j + 1], at + 1)
         det = a * d - b * b
         r = pl.reciprocal(det, approx=True)
         r = r * (2.0 - det * r)
         r = r * (2.0 - det * r)
         ar, br, dr = a * r, b * r, d * r
-        pair = (row == j) | (row == j + 1)
-        m1 = jnp.where(pair, 0.0, cols[j])
-        m2 = jnp.where(pair, 0.0, cols[j + 1])
-        same = jnp.where(row == j, dr, jnp.where(row == j + 1, ar, same))
-        other = jnp.where(pair, br, other)
+        pair = (row == at) | (row == at + 1)
+        m1, m2 = list(cols[j]), list(cols[j + 1])
+        m1[home] = jnp.where(pair, 0.0, m1[home])
+        m2[home] = jnp.where(pair, 0.0, m2[home])
+        same[home] = jnp.where(row == at, dr, jnp.where(row == at + 1, ar, same[home]))
+        other[home] = jnp.where(pair, br, other[home])
+
+        def reduced(v):
+            x, y = take(v, at), take(v, at + 1)
+            first, second = dr * x - br * y, ar * y - br * x
+            return [v[t] - m1[t] * first - m2[t] * second for t in tiles]
+
         for i in range(j + 2, W):
-            x, y = cols[i][j:j + 1, :], cols[i][j + 1:j + 2, :]
-            cols[i] = cols[i] - m1 * (dr * x - br * y) - m2 * (ar * y - br * x)
-        x, y = right[j:j + 1, :], right[j + 1:j + 2, :]
-        arw, brw, drw = widen_lanes(ar), widen_lanes(br), widen_lanes(dr)
-        right = right - widen_lanes(m1) * (drw * x - brw * y) - widen_lanes(m2) * (arw * y - brw * x)
-    even = lax.broadcasted_iota(jnp.int32, (W, size), 0) % 2 == 0
-    swapped = jnp.where(even, pltpu.roll(right, W - 1, 0), pltpu.roll(right, 1, 0))
-    return right * widen_lanes(same) - swapped * widen_lanes(other)
+            cols[i] = reduced(cols[i])
+        right = [reduced(v) for v in right]
+    even = row % 2 == 0
+    done = [[v[t] * same[t] - jnp.where(even, pltpu.roll(v[t], 7, 0), pltpu.roll(v[t], 1, 0)) * other[t] for t in tiles]
+            for v in right]
+    return jnp.concatenate([jnp.concatenate(v, axis=0) for v in done], axis=1)
 
 
 def six_terms(left, right):
@@ -96,10 +105,9 @@
         sweep_apply(cov, lhs, rhs, start - W)
         cov[pl.ds(start, W), :] = jnp.zeros((W, size), F32)
         rolled = pltpu.roll(panel, size - start, 1)
-        cols = [jnp.broadcast_to(rolled[:, i:i + 1], (W, 128)) for i in range(W)]
         inside = (lane >= start) & (lane < start + W)
         left = jnp.where(inside, jnp.where(lane - start == row, -1.0, 0.0), panel)
-        right = eliminate(cols, left)
+        right = eliminate(rolled, left)
         after = ((k + 1) % (size // W)) * W
         lhs[...], rhs[...] = six_terms(left, right)
         ahead, _ = six_terms(pltpu.roll(left, size - after, 1)[:, :128], left)
@@ -329,15 +337,17 @@
     pl.semaphore_wait(barrier, nrows + ncols - 2)
     core0 = to_core(0)
     select(1)
+    core1 = to_core(1)
     sums0 = to_chips(0, core0)
-    core1 = to_core(1)
     lines0 = along_line(0, sums0)
     first0 = spread(0, 0)
+    sums1 = to_chips(1, core1)
     notes = [put(note_src, note_slots.at[d - 1], nsum_s.at[d - 1], nsum_r.at[d - 1], flip(me, d), col)
              for d in range(1, nrows)]
     planes0, pairs0 = spread_lines(0, lines0, first0)
+    lines1 = along_line(1, sums1)
+    later = [lines1, spread(1, 0)]
     relay_all(0, planes0, pairs0)
-    sums1 = to_chips(1, core1)
     finish(0, planes0, pairs0)
     total = note_src[...]
     for d in range(1, nrows):
@@ -348,17 +358,13 @@
                   for d in range(1, ncols)]
     for copy in pairs0:
         copy.wait_recv()
-    later = []
 
     def beside(stage):
         if stage == 0:
-            lines1 = along_line(1, sums1)
-            later.extend([lines1, spread(1, 0)])
+            later[:] = spread_lines(1, *later)
         elif stage == 1:
-            later[:] = spread_lines(1, *later)
+            relay_all(1, *later)
         elif stage == 2:
-            relay_all(1, *later)
-        elif stage == 3:
             finish(1, *later)
         elif stage == 5:
             for copy in later[1] + note_lines:

time: 53.4 us -> 52.5 us (0.983)
  Pallas kernels: 53.2 us -> 52.3 us
    pallas_call x1, Pallas kernels: 38.8 us -> 37.5 us  [on_device(): pl.pallas_call(functools.partial(share_kernel, nrows, ncols), out_shape=(...]
where the time goes in v5:
time: 52.5 us; the launch traced here: 52.3 us
  Pallas kernels  52.3 us (100%)
    pallas_call x1, Pallas kernels, on_device(): pl.pallas_call(functools.partial(share_kernel, nrows, ncols), out_shape=(...  37.5 us
    pallas_call x1, Pallas kernels, on_device(): pl.pallas_call(functools.partial(second_kernel, nrows, ncols, taper_mask....  14.8 us

profile of v5, /device:TPU:0, one launch (start us, length us, event | category | flops | bytes accessed | tf_op | source)
XLA Modules:
  0.0 52.3 jit_solution(3027952650933616806)
XLA Ops:
  0.0 37.5 %shard_map.64 = (f32[2,4,8,8,1024]{4,3,2,1,0:T(8,128)S(1)}, f32[4,8,128]{2,1,0:T(8,128)S(1)}, f32[256,256]{1,0:T(8,128)S(1)}, f32[128,1024]{1,0:T(8,128)S(1)}, b...) custom-call(f32[128,1024]{1,0:T(8,128)} %x_hbm.1, ...), custom_call_target="tpu_custom_call" | custom-call | tf_op jit(solution)/shard_map/pallas_call | solution.py:444
  37.5 14.8 %shard_map.65 = f32[128,1024]{1,0:T(8,128)} custom-call(f32[2,4,8,8,1024]{4,3,2,1,0:T(8,128)S(1)} %get-tuple-element.14.g_ref, f32[4,8,128]{2,1,0:T(8,128)S(1)} %get-tuple-element.15.note_ref, f32[256,256]{1,0:T(8,128)S(1)} %get-tuple-element.16.inv_ref, f32[128,1024]{1,0:T(8,128)S(1)} %get-tuple-element.17.x1_ref, ...), custom_call_target="tpu_custom_call" | custom-call | tf_op jit(solution)/shard_map/pallas_call | solution.py:482

commit v6 on v3

--- a/solution.py
+++ b/solution.py
@@ -146,8 +146,8 @@
     aux_ref[6:8, :] = var_ref[...]
     push_hi[...], push_lo[...] = split2(column_of(val_ref[0:1, :], eye_of(count)) - m0 - 0.5 * a0)
     steps = count // W
-    cuts = [0, steps // 4, steps // 2, 13 * steps // 16, steps]
-    for k in range(4):
+    cuts = [0, steps // 4, 5 * steps // 8, steps]
+    for k in range(3):
         sweep_inverse(inv_ref, cuts[k], cuts[k + 1])
         beside(k + 1)
     x = x_ref[...]
@@ -293,15 +293,17 @@
     pl.semaphore_wait(barrier, nrows + ncols - 2)
     core0 = to_core(0)
     select(1)
+    core1 = to_core(1)
     sums0 = to_chips(0, core0)
-    core1 = to_core(1)
     lines0 = along_line(0, sums0)
     first0 = spread(0, 0)
+    sums1 = to_chips(1, core1)
     notes = [put(note_src, note_slots.at[d - 1], nsum_s.at[d - 1], nsum_r.at[d - 1], flip(me, d), col)
              for d in range(1, nrows)]
     planes0, pairs0 = spread_lines(0, lines0, first0)
+    lines1 = along_line(1, sums1)
+    later = [lines1, spread(1, 0)]
     relay_all(0, planes0, pairs0)
-    sums1 = to_chips(1, core1)
     finish(0, planes0, pairs0)
     total = note_src[...]
     for d in range(1, nrows):
@@ -312,17 +314,13 @@
                   for d in range(1, ncols)]
     for copy in pairs0:
         copy.wait_recv()
-    later = []
 
     def beside(stage):
         if stage == 0:
-            lines1 = along_line(1, sums1)
-            later.extend([lines1, spread(1, 0)])
+            later[:] = spread_lines(1, *later)
         elif stage == 1:
-            later[:] = spread_lines(1, *later)
+            relay_all(1, *later)
         elif stage == 2:
-            relay_all(1, *later)
-        elif stage == 3:
             finish(1, *later)
         elif stage == 5:
             for copy in later[1] + note_lines:

time: 52.8 us -> 50.3 us (0.953)
  Pallas kernels: 52.7 us -> 50.1 us
    pallas_call x1, Pallas kernels: 38.6 us -> 36.1 us  [on_device(): pl.pallas_call(functools.partial(share_kernel, nrows, ncols), out_shape=(...]
where the time goes in v6:
time: 50.3 us; the launch traced here: 50.1 us
  Pallas kernels  50.1 us (100%)
    pallas_call x1, Pallas kernels, on_device(): pl.pallas_call(functools.partial(share_kernel, nrows, ncols), out_shape=(...  36.1 us
    pallas_call x1, Pallas kernels, on_device(): pl.pallas_call(functools.partial(second_kernel, nrows, ncols, taper_mask....  14.1 us

profile of v6, /device:TPU:0, one launch (start us, length us, event | category | flops | bytes accessed | tf_op | source)
XLA Modules:
  0.0 50.1 jit_solution(11537904193133138146)
XLA Ops:
  0.0 36.1 %shard_map.64 = (f32[2,4,8,8,1024]{4,3,2,1,0:T(8,128)S(1)}, f32[4,8,128]{2,1,0:T(8,128)S(1)}, f32[256,256]{1,0:T(8,128)S(1)}, f32[128,1024]{1,0:T(8,128)S(1)}, b...) custom-call(f32[128,1024]{1,0:T(8,128)} %x_hbm.1, ...), custom_call_target="tpu_custom_call" | custom-call | tf_op jit(solution)/shard_map/pallas_call | solution.py:397
  36.1 14.1 %shard_map.65 = f32[128,1024]{1,0:T(8,128)} custom-call(f32[2,4,8,8,1024]{4,3,2,1,0:T(8,128)S(1)} %get-tuple-element.14.g_ref, f32[4,8,128]{2,1,0:T(8,128)S(1)} %get-tuple-element.15.note_ref, f32[256,256]{1,0:T(8,128)S(1)} %get-tuple-element.16.inv_ref, f32[128,1024]{1,0:T(8,128)S(1)} %get-tuple-element.17.x1_ref, ...), custom_call_target="tpu_custom_call" | custom-call | tf_op jit(solution)/shard_map/pallas_call | solution.py:434

commit v7 on v6

--- a/solution.py
+++ b/solution.py
@@ -39,10 +39,13 @@
     return mm(a[0], b[0], dims) + (mm(a[0], b[1], dims) + mm(a[1], b[0], dims))
 
 
-def sweep_inverse(cov, begin=0, end=None):
+def sweep_inverse(cov, rhs, begin=0, end=None):
     size = cov.shape[0]
     lane = lax.broadcasted_iota(jnp.int32, (W, size), 1)
     row = lax.broadcasted_iota(jnp.int32, (W, size), 0)
+    line = lax.broadcasted_iota(jnp.int32, (1, size), 1)
+    if begin == 0:
+        rhs[...] = jnp.zeros(rhs.shape, BF16)
     row_small = lax.broadcasted_iota(jnp.int32, (W, 128), 0)
 
     def body(k, carry):
@@ -52,6 +55,11 @@
         cols = [jnp.broadcast_to(rolled[:, i:i + 1], (W, 128)) for i in range(W)]
         inside = (lane >= start) & (lane < start + W)
         left = jnp.where(inside, jnp.where(lane - start == row, -1.0, 0.0), panel)
+        group = pl.multiple_of((start // 128) * 128, 128)
+        cov[pl.ds(start, W), :] = jnp.where(inside, left, 0.0)
+        own = line[:, :128] + group
+        a1, a2, a3 = split3(jnp.where((own >= start) & (own < start + W), cov[:, pl.ds(group, 128)], 0.0))
+        lhs = [jnp.concatenate(two, axis=1) for two in ((a1, a1), (a2, a1), (a2, a3))]
         right = left
         scale = jnp.zeros((W, 128), F32)
         for j in range(W):
@@ -65,15 +73,13 @@
             wide_inv = jnp.concatenate([inv] * (size // 128), axis=1)
             right = right - wide * (right[j:j + 1, :] * wide_inv)
         right = right * jnp.concatenate([scale] * (size // 128), axis=1)
-        a1, a2, a3 = split3(left)
-        b1, b2, b3 = split3(right)
-        lhs = jnp.concatenate([a1, a1, a2, a1, a2, a3], axis=0)
-        rhs = jnp.concatenate([b1, b2, b1, b3, b2, b1], axis=0)
-        change = mm(lhs, rhs, TN)
-        r_ids = lax.broadcasted_iota(jnp.int32, (size, size), 0)
-        c_ids = lax.broadcasted_iota(jnp.int32, (size, size), 1)
-        hit = ((r_ids >= start) & (r_ids < start + W)) | ((c_ids >= start) & (c_ids < start + W))
-        cov[...] = jnp.where(hit, 0.0, cov[...]) - change
+        for t, term in enumerate(split3(right)):
+            rhs[t, pl.ds(pl.multiple_of(start - group, W), W), :] = term
+        b1, b2, b3 = rhs[0], rhs[1], rhs[2]
+        change = (mm(lhs[0], jnp.concatenate([b1, b2], axis=0), NN)
+                  + (mm(lhs[1], jnp.concatenate([b1, b3], axis=0), NN)
+                     + mm(lhs[2], jnp.concatenate([b2, b1], axis=0), NN)))
+        cov[...] = jnp.where((line >= start) & (line < start + W), 0.0, cov[...]) - change
         return carry
 
     lax.fori_loop(begin, size // W if end is None else end, body, 0)
@@ -124,7 +130,7 @@
 
 
 def first_batch(nrows, ncols, g_ref, x_ref, rows_ref, owner_ref, mask_ref, val_ref, var_ref,
-                inv_ref, x1_ref, anom_hi, anom_lo, push_hi, push_lo, aux_ref, beside):
+                inv_ref, x1_ref, anom_hi, anom_lo, push_hi, push_lo, aux_ref, rhs, beside):
     rows, members = x_ref.shape
     count = rows_ref.shape[1]
     nblk = mask_ref.shape[2]
@@ -148,7 +154,7 @@
     steps = count // W
     cuts = [0, steps // 4, 5 * steps // 8, steps]
     for k in range(3):
-        sweep_inverse(inv_ref, cuts[k], cuts[k + 1])
+        sweep_inverse(inv_ref, rhs, cuts[k], cuts[k + 1])
         beside(k + 1)
     x = x_ref[...]
     taper = taper_of(my_positions(rows, count, ncols), aux_ref[0:1, :], aux_ref[2:3, :], local_len)
@@ -172,7 +178,7 @@
 
 def share_kernel(nrows, ncols, x_hbm, rows_hbm, owner_hbm, mask_hbm, val_hbm, var_hbm, g_ref, note_ref,
                  inv_ref, x1_ref, anom_hi, anom_lo, push_hi, push_lo, aux_ref,
-                 x_ref, rows_ref, owner_ref, mask_ref, val_ref, var_ref, load, src, core_slot, part, slots,
+                 rhs, x_ref, rows_ref, owner_ref, mask_ref, val_ref, var_ref, load, src, core_slot, part, slots,
                  note_src, note_slots, core_s, core_r, sum_s, sum_r, line_s, line_r, plane_s, plane_r, pair_s, pair_r,
                  nsum_s, nsum_r, nline_s, nline_r):
     loads = [pltpu.make_async_copy(source, target, load.at[k]) for k, (source, target) in enumerate((
@@ -327,13 +333,13 @@
                 copy.wait_recv()
 
     first_batch(nrows, ncols, g_ref, x_ref, rows_ref, owner_ref, mask_ref, val_ref, var_ref,
-                inv_ref, x1_ref, anom_hi, anom_lo, push_hi, push_lo, aux_ref, beside)
+                inv_ref, x1_ref, anom_hi, anom_lo, push_hi, push_lo, aux_ref, rhs, beside)
     for copy in sent:
         copy.wait_send()
 
 
 def second_kernel(nrows, ncols, nblk, g_ref, note_ref, inv_ref, x1_ref, anom_hi, anom_lo, push_hi, push_lo, aux_ref,
-                  out_ref, g1, cov):
+                  out_ref, g1, cov, rhs):
     rows, members = x1_ref.shape
     count = inv_ref.shape[0]
     local_len = float(rows * nrows * ncols // 4)
@@ -350,7 +356,7 @@
     a1 = g - m1
     a12 = split2(a1)
     covariance(a12, aux_ref[7:8, :], cov)
-    sweep_inverse(cov)
+    sweep_inverse(cov, rhs)
     push = split2(column_of(aux_ref[5:6, :], eye) - m1 - 0.5 * a1)
     x = x1_ref[...]
     taper = taper_of(my_positions(rows, count, ncols), aux_ref[1:2, :], aux_ref[3:4, :], local_len)
@@ -390,6 +396,7 @@
         jax.ShapeDtypeStruct((8, count), F32),
     )
     limit = 40 * 2**20
+    terms = [pltpu.VMEM((3, 128, count), BF16)]
     if nrows == 8 and ncols & (ncols - 1) == 0 and per_dev % (8 * nrows) == 0:
         q = per_dev // nrows
         half = nrows // 2
@@ -402,7 +409,7 @@
             ) + kept,
             in_specs=[HBM] * 6,
             out_specs=(VMEM,) * 9,
-            scratch_shapes=[
+            scratch_shapes=terms + [
                 pltpu.VMEM(ensemble.shape, F32),
                 pltpu.VMEM(obs_rows.shape, jnp.int32),
                 pltpu.SMEM(owner.shape, jnp.int32),
@@ -429,6 +436,7 @@
             out_shape=kept,
             in_specs=[VMEM] * 3 + [SMEM] * 2 + [VMEM] * 2,
             out_specs=(VMEM,) * 7,
+            scratch_shapes=terms,
             compiler_params=pltpu.CompilerParams(vmem_limit_bytes=limit),
         )(shared, ensemble, obs_rows, owner, taper_mask, obs_value, obs_var)
     return pl.pallas_call(
@@ -436,7 +444,7 @@
         out_shape=jax.ShapeDtypeStruct((rows, members), F32),
         in_specs=[VMEM] * 9,
         out_specs=VMEM,
-        scratch_shapes=[pltpu.VMEM((count, members), F32), pltpu.VMEM((count, count), F32)],
+        scratch_shapes=[pltpu.VMEM((count, members), F32), pltpu.VMEM((count, count), F32)] + terms,
         compiler_params=pltpu.CompilerParams(vmem_limit_bytes=limit),
     )(shared, note, *held)
 

time: 50.3 us -> 52.5 us (1.044)
  Pallas kernels: 50.1 us -> 52.4 us
    pallas_call x1, Pallas kernels: 14.1 us -> 15.4 us  [on_device(): pl.pallas_call(functools.partial(second_kernel, nrows, ncols, taper_mask....]
    pallas_call x1, Pallas kernels: 36.1 us -> 37 us  [on_device(): pl.pallas_call(functools.partial(share_kernel, nrows, ncols), out_shape=(...]
where the time goes in v7:
time: 52.5 us; the launch traced here: 52.4 us
  Pallas kernels  52.4 us (100%)
    pallas_call x1, Pallas kernels, on_device(): pl.pallas_call(functools.partial(share_kernel, nrows, ncols), out_shape=(...  37 us
    pallas_call x1, Pallas kernels, on_device(): pl.pallas_call(functools.partial(second_kernel, nrows, ncols, taper_mask....  15.4 us

profile of v7, /device:TPU:0, one launch (start us, length us, event | category | flops | bytes accessed | tf_op | source)
XLA Modules:
  0.0 52.4 jit_solution(17185637159991966740)
XLA Ops:
  0.0 37.0 %shard_map.64 = (f32[2,4,8,8,1024]{4,3,2,1,0:T(8,128)S(1)}, f32[4,8,128]{2,1,0:T(8,128)S(1)}, f32[256,256]{1,0:T(8,128)S(1)}, f32[128,1024]{1,0:T(8,128)S(1)}, b...) custom-call(f32[128,1024]{1,0:T(8,128)} %x_hbm.1, ...), custom_call_target="tpu_custom_call" | custom-call | tf_op jit(solution)/shard_map/pallas_call | solution.py:404
  37.0 15.4 %shard_map.65 = f32[128,1024]{1,0:T(8,128)} custom-call(f32[2,4,8,8,1024]{4,3,2,1,0:T(8,128)S(1)} %get-tuple-element.14.g_ref, f32[4,8,128]{2,1,0:T(8,128)S(1)} %get-tuple-element.15.note_ref, f32[256,256]{1,0:T(8,128)S(1)} %get-tuple-element.16.inv_ref, f32[128,1024]{1,0:T(8,128)S(1)} %get-tuple-element.17.x1_ref, ...), custom_call_target="tpu_custom_call" | custom-call | tf_op jit(solution)/shard_map/pallas_call | solution.py:442
